TPU v7x, 256 devices: a whole 4x4x8 slice. The times are simulated.
256 devices in a mesh: row: 16 (over y, z_lo, core), col: 16 (over z_hi, x).
Axes of the slice: x: 4, y: 4, z: 8 (z_hi: 4, z_lo: 2; z = z_hi * 2 + z_lo), core: 2. Of those that a mesh axis runs over, the one named last changes fastest.
Arguments:
- pair: bfloat16 [512, 512, 128], P('row', 'col'), may hold values from -6 to 6
- cotangent: bfloat16 [512, 512, 128], P('row', 'col'), may hold values from -6 to 6
- contact: int32 [4, 4], replicated, may hold values 0 or 1
- chain: int32 [512], replicated, may hold values from 0 to 3, never falling along the last dimension, each value on 1 to 256 neighbouring positions
- gain_in: float32 [128], replicated, may hold values from 0.1 to 1.9
- output_norm_gain: float32 [128], replicated, may hold values from 0.1 to 1.9
- w_in: bfloat16 [128, 512], replicated, may hold values from -0.5 to 0.5
- w_gate: bfloat16 [128, 128], replicated, may hold values from -0.5 to 0.5
- w_out: bfloat16 [128, 128], replicated, may hold values from -0.5 to 0.5
Outputs:
- update: bfloat16 [512, 512, 128], P('row', 'col')
- grad_pair: float32 [512, 512, 128], P('row', 'col')
- grad_w_in: float32 [128, 512], replicated
- grad_w_gate: float32 [128, 128], replicated
- grad_w_out: float32 [128, 128], replicated
- grad_gain_in: float32 [128], replicated
- output_norm_gain_gradient: float32 [128], replicated
All inputs are finite; a program needn't handle non-finite values.
Results may differ from a plain program's by a relative error of at most 0.014.
Values may be sent and summed in bfloat16 or wider, within the bound.
No kernel may reach another device: no remote copies, remote signals or barrier semaphores. Data moves between devices by JAX's collectives and lax.ppermute only.
A program may use at most 128 MiB of HBM per device.

v0:
```python
import jax
import jax.numpy as jnp
from jax import lax
from jax.sharding import PartitionSpec as P

BLOCK = 128


EPS = 1e-05
HIGH = lax.Precision.HIGHEST


def normalized_product(values):
    mean = jnp.mean(values, axis=-1, keepdims=True)
    centred = values - mean
    rstd = lax.rsqrt(jnp.mean(centred * centred, axis=-1, keepdims=True) + EPS)
    return (centred * rstd, rstd)


def norm_backward_step(dnorm, nhat, rstd):
    first = jnp.mean(dnorm, axis=-1, keepdims=True)
    second = jnp.mean(dnorm * nhat, axis=-1, keepdims=True)
    return rstd * (dnorm - first - nhat * second)


def project_in(pair, gain_in, w_in, mask, hidden):
    nhat, rstd = normalized_product(pair.astype(jnp.float32))
    normed = (nhat * gain_in).astype(jnp.bfloat16)
    proj = jnp.einsum("pqc,cd->pqd", normed, w_in, preferred_element_type=jnp.float32)
    weight = mask[..., None]
    sig_a = jax.nn.sigmoid(proj[..., hidden : 2 * hidden])
    sig_b = jax.nn.sigmoid(proj[..., 3 * hidden :])
    left = (sig_a * proj[..., :hidden] * weight).astype(jnp.bfloat16)
    right = (sig_b * proj[..., 2 * hidden : 3 * hidden] * weight).astype(jnp.bfloat16)
    return (nhat, rstd, normed, proj, left, right)


def project_back(grad_left, grad_right, normed, proj, mask, w_in, hidden):
    weight = mask[..., None]
    fleft = grad_left.astype(jnp.float32) * weight
    fright = grad_right.astype(jnp.float32) * weight
    val_a = proj[..., :hidden]
    sig_a = jax.nn.sigmoid(proj[..., hidden : 2 * hidden])
    val_b = proj[..., 2 * hidden : 3 * hidden]
    sig_b = jax.nn.sigmoid(proj[..., 3 * hidden :])
    dproj = jnp.concatenate(
        [
            fleft * sig_a,
            fleft * val_a * sig_a * (1.0 - sig_a),
            fright * sig_b,
            fright * val_b * sig_b * (1.0 - sig_b),
        ],
        axis=-1,
    )
    grad_w = jnp.einsum("pqc,pqd->cd", normed.astype(jnp.float32), dproj, precision=HIGH)
    dnormed = jnp.einsum("pqd,cd->pqc", dproj, w_in.astype(jnp.float32), precision=HIGH)
    return (dnormed, grad_w)


def output_pass(triangle_product, normed, cotangent, output_norm_gain, w_gate, w_out):
    gate = jax.nn.sigmoid(
        jnp.einsum("pqc,cd->pqd", normed, w_gate, preferred_element_type=jnp.float32)
    )
    centred_scaled_input, input_reciprocal_deviation = normalized_product(triangle_product)
    input_normed_rows = (centred_scaled_input * output_norm_gain).astype(jnp.bfloat16)
    outp = jnp.einsum("pqh,hc->pqc", input_normed_rows, w_out, preferred_element_type=jnp.float32)
    update = (gate * outp).astype(jnp.bfloat16)
    dyf = cotangent.astype(jnp.float32)
    dout = dyf * gate
    dgpre = dyf * outp * gate * (1.0 - gate)
    grad_w_out = jnp.einsum(
        "pqh,pqc->hc", input_normed_rows.astype(jnp.float32), dout, precision=HIGH
    )
    normed_input_gradient = jnp.einsum(
        "pqc,hc->pqh", dout, w_out.astype(jnp.float32), precision=HIGH
    )
    output_norm_gain_gradient = jnp.sum(normed_input_gradient * centred_scaled_input, axis=(0, 1))
    product_gradient = norm_backward_step(
        normed_input_gradient * output_norm_gain, centred_scaled_input, input_reciprocal_deviation
    ).astype(jnp.bfloat16)
    grad_w_gate = jnp.einsum("pqc,pqd->cd", normed.astype(jnp.float32), dgpre, precision=HIGH)
    dnormed = jnp.einsum("pqd,cd->pqc", dgpre, w_gate.astype(jnp.float32), precision=HIGH)
    return (update, product_gradient, dnormed, grad_w_out, output_norm_gain_gradient, grad_w_gate)


def tile_mask(contact, chain, row_start, rows_here, col_start, cols_here):
    blocks = contact.shape[0]
    row_pos = row_start + jnp.arange(rows_here, dtype=jnp.int32)
    col_pos = col_start + jnp.arange(cols_here, dtype=jnp.int32)
    labels = jnp.arange(blocks, dtype=jnp.int32)
    onehot_row = (row_pos[:, None] // BLOCK == labels[None, :]).astype(jnp.float32)
    onehot_col = (col_pos[:, None] // BLOCK == labels[None, :]).astype(jnp.float32)
    listed_col = jnp.dot(onehot_col, contact.astype(jnp.float32), precision=HIGH)
    listed = jnp.dot(onehot_row, listed_col.T, precision=HIGH)
    chain_row = lax.dynamic_slice_in_dim(chain, row_start, rows_here)
    chain_col = lax.dynamic_slice_in_dim(chain, col_start, cols_here)
    same = (chain_row[:, None] == chain_col[None, :]).astype(jnp.float32)
    return jnp.maximum(listed, same)


def on_device(pair, cotangent, contact, chain, gain_in, output_norm_gain, w_in, w_gate, w_out):
    rows_here = pair.shape[0]
    cols_here = pair.shape[1]
    hidden = w_out.shape[0]
    row_start = lax.axis_index("row") * rows_here
    col_start = lax.axis_index("col") * cols_here
    mask = tile_mask(contact, chain, row_start, rows_here, col_start, cols_here)
    nhat, rstd, normed, proj, left, right = project_in(pair, gain_in, w_in, mask, hidden)
    left_rows = lax.all_gather(left, "col", axis=1, tiled=True)
    triangle_product = lax.psum_scatter(
        jnp.einsum("kih,kjh->ijh", left_rows, right, preferred_element_type=jnp.float32),
        "row",
        scatter_dimension=0,
        tiled=True,
    )
    update, product_gradient, dnorm_out, grad_w_out, output_norm_gain_gradient, grad_w_gate = (
        output_pass(triangle_product, normed, cotangent, output_norm_gain, w_gate, w_out)
    )
    left_back = lax.all_gather(left, "col", axis=1, tiled=True)
    dproduct_all = lax.all_gather(product_gradient, "row", axis=0, tiled=True)
    grad_right = jnp.einsum(
        "kih,ijh->kjh", left_back, dproduct_all, preferred_element_type=jnp.float32
    ).astype(jnp.bfloat16)
    grad_left_swapped = lax.psum_scatter(
        jnp.einsum("qjh,kjh->qkh", dproduct_all, right, preferred_element_type=jnp.float32).astype(
            jnp.bfloat16
        ),
        "col",
        scatter_dimension=0,
        tiled=True,
    ).astype(jnp.float32)
    grad_left = jnp.transpose(grad_left_swapped, (1, 0, 2)).astype(jnp.bfloat16)
    dnorm_in, grad_w_in = project_back(grad_left, grad_right, normed, proj, mask, w_in, hidden)
    dnormed = dnorm_out + dnorm_in
    grad_gain_in = jnp.sum(dnormed * nhat, axis=(0, 1))
    grad_pair = norm_backward_step(dnormed * gain_in, nhat, rstd)
    totals = lax.psum(
        (grad_w_in, grad_w_gate, grad_w_out, grad_gain_in, output_norm_gain_gradient),
        ("row", "col"),
    )
    return (update, grad_pair, totals[0], totals[1], totals[2], totals[3], totals[4])


def solution(mesh):
    return jax.shard_map(
        on_device,
        mesh=mesh,
        in_specs=(P("row", "col", None), P("row", "col", None), P(), P(), P(), P(), P(), P(), P()),
        out_specs=(P("row", "col", None), P("row", "col", None), P(), P(), P(), P(), P()),
        check_vma=False,
    )
```

profile of v0, /device:TPU:1, one launch (start us, length us, event | category | flops | bytes accessed | tf_op | source)
XLA Modules:
  0.0 730.4 jit_solution(2967407663969828167)
XLA Ops:
  8.4 1.3 fusion.16
  11.5 1.4 fusion.35
  14.3 1.4 copy.34
  15.7 85.2 %all-gather.3.cloned.1.call-done = bf16[32,512,128]{2,1,0:T(8,128)(2,1)} async-done(((bf16[32,32,128]{2,1,0:T(8,128)(2,1)}), bf16[32,512,128]{2,1,0:T(8,128)(2,1)}) %all-gather.3.cloned.1.call-update) | async-done | bytes 4194320 | tf_op jit(solution)/shard_map/all_gather | solution.py:109
  101.0 7.9 %copy.32 = bf16[32,512,128]{1,0,2:T(8,128)(2,1)} copy(bf16[32,512,128]{2,1,0:T(8,128)(2,1)} %all-gather.3.cloned.1.call-done) | data formatting | bytes 8388608 | tf_op jit(solution)/shard_map/all_gather | solution.py:109
  108.9 6.7 convolution_bitcast_fusion
  115.6 11.0 %copy.33 = f32[512,32,128]{2,1,0:T(8,128)} copy(f32[512,32,128]{0,1,2:T(8,128)} %convolution_bitcast_fusion) | data formatting | bytes 16777216 | tf_op jit(solution)/shard_map/kih,kjh->ijh/transpose | solution.py:111
  126.6 97.2 %reduce-scatter.3.cloned.1.call-done = f32[32,32,128]{2,1,0:T(8,128)} async-done(((f32[512,32,128]{2,1,0:T(8,128)}), f32[32,32,128]{2,1,0:T(8,128)}) %reduce-scatter.3.cloned.1.call-update) | async-done | bytes 524304 | tf_op jit(solution)/shard_map/reduce_scatter | solution.py:110
  225.1 1.4 multiply_reduce_fusion.2
  226.6 1.5 fusion.38
  228.1 2.1 multiply_convert_fusion.1
  230.2 2.2 multiply_reduce_fusion
  232.4 2.0 multiply_convert_fusion
  234.5 40.6 %all-gather.5.cloned.1.call-done = bf16[512,32,128]{2,1,0:T(8,128)(2,1)} async-done(((bf16[32,32,128]{2,1,0:T(8,128)(2,1)}), bf16[512,32,128]{2,1,0:T(8,128)(2,1)}) %all-gather.5.cloned.1.call-update) | async-done | bytes 4194320 | tf_op jit(solution)/shard_map/all_gather | solution.py:120
  275.1 8.6 %copy.37 = bf16[512,32,128]{0,1,2:T(8,128)(2,1)} copy(bf16[512,32,128]{2,1,0:T(8,128)(2,1)} %all-gather.5.cloned.1.call-done) | data formatting | bytes 8388608 | tf_op jit(solution)/shard_map/all_gather | solution.py:120
  283.7 5.7 fusion.58
  289.4 7.9 %copy.36 = bf16[128,32,512]{0,2,1:T(8,128)(2,1)} copy(bf16[128,32,512]{2,1,0:T(8,128)(2,1)} %fusion.58) | data formatting | bytes 8388608 | tf_op jit(solution)/shard_map/qjh,kjh->qkh/dot_general | solution.py:125
  297.6 2.6 convolution_bitcast_fusion.1
  300.2 2.6 convolution_bitcast_fusion.2
  302.7 2.4 fusion.40
  305.1 3.4 fusion.59
  308.6 2.0 copy.39
  310.6 81.8 %reduce-scatter.5.cloned.1.call-done = bf16[32,32,128]{2,0,1:T(8,128)(2,1)} async-done(((bf16[512,32,128]{2,0,1:T(8,128)(2,1)}), bf16[32,32,128]{2,0,1:T(8,128)(2,1)}) %reduce-scatter.5.cloned.1.call-update) | async-done | bytes 262160 | tf_op jit(solution)/shard_map/reduce_scatter | solution.py:124
  392.4 1.5 fusion.30
  395.0 1.9 fusion.4
  396.9 2.7 fusion.15
  399.7 74.5 %all-reduce = (f32[128]{0:T(128)}, f32[128]{0:T(128)}) all-reduce(f32[128]{0:T(128)S(1)} %get-tuple-element.9, f32[128]{0:T(128)S(1)} %copy-done.22), channel_id=1, replica_groups=mesh['row'=16,'col'=16] {'row','col'}, use_global_device_ids=true, to_apply=%region_14.15 | all-reduce | flops 256 | bytes 2048 | tf_op jit(solution)/shard_map/psum | solution.py:137
  474.2 1.4 fusion.14
  475.6 243.6 %all-reduce.4.cloned.1.call-done = (f32[128,512]{1,0:T(8,128)}, f32[128,128]{1,0:T(8,128)}, f32[128,128]{1,0:T(8,128)}) async-done(((f32[128,512]{1,0:T(8,128)}, f32[128,128]{1,0:T(8,128)}, f32[128,128]{1,0:T(8,128)}), (f32[128,512]{1,0:T(8,128)}, f32[128,128]{1,0:T(8,128)}, f32[128,128]{1,0:T(8,128)})) %all-reduce.4.cloned.1.call-update) | async-done | bytes 393232 | tf_op jit(solution)/shard_map/psum | solution.py:137
  719.3 1.7 copy.43
  720.9 1.5 copy.44
  722.4 1.5 copy.45
  (71 shorter events, 7.1 us)
Async XLA Ops:
  7.2 4.4 copy-start
  7.2 93.8 %all-gather.3.cloned.1.call-start = ((), (), s32[]{:S(2)}) async-start(), calls=%async_computation.2 | async-start | bytes 4456448 | tf_op jit(solution)/shard_map/all_gather | solution.py:109
  8.4 5.8 copy-start.12
  9.8 4.5 copy-start.14
  13.1 1.1 copy-start.18
  14.2 209.6 %reduce-scatter.3.cloned.1.call-start = ((), (), s32[]{:S(2)}) async-start(), calls=%async_computation.3 | async-start | bytes 8912896 | tf_op jit(solution)/shard_map/reduce_scatter | solution.py:110
  15.7 93.1 %copy-start.3 = (bf16[32,32,128]{1,0,2:T(8,128)(2,1)}, bf16[32,32,128]{1,0,2:T(8,128)(2,1)S(1)}, u32[]{:S(2)}) copy-start(bf16[32,32,128]{1,0,2:T(8,128)(2,1)S(1)} %copy.34) | copy-start | bytes 786436
  126.6 100.0 %copy-start.17 = (bf16[128,128]{1,0:T(8,128)(2,1)S(1)}, bf16[128,128]{1,0:T(8,128)(2,1)}, u32[]{:S(2)}) copy-start(bf16[128,128]{1,0:T(8,128)(2,1)} %param.17) | copy-start | bytes 98308
  126.6 100.0 %copy-start.19 = (f32[128]{0:T(128)S(1)}, f32[128]{0:T(128)}, u32[]{:S(2)}) copy-start(f32[128]{0:T(128)} %param.14) | copy-start | bytes 1540
  126.6 101.5 %copy-start.4 = (bf16[32,32,128]{2,1,0:T(8,128)(2,1)S(1)}, bf16[32,32,128]{2,1,0:T(8,128)(2,1)}, u32[]{:S(2)}) copy-start(bf16[32,32,128]{2,1,0:T(8,128)(2,1)} %param.9) | copy-start | bytes 786436
  126.6 148.5 %all-gather.5.cloned.1.call-start = ((), (), s32[]{:S(2)}) async-start(), calls=%async_computation.4 | async-start | bytes 4456448 | tf_op jit(solution)/shard_map/all_gather | solution.py:120
  223.8 6.5 copy-start.2
  226.6 5.8 copy-start.11
  228.1 2.1 copy-start.5
  234.4 157.9 %reduce-scatter.5.cloned.1.call-start = ((), (), s32[]{:S(2)}) async-start(), calls=%async_computation.5 | async-start | bytes 4456448 | tf_op jit(solution)/shard_map/reduce_scatter | solution.py:124
  297.3 421.9 %all-reduce.4.cloned.1.call-start = ((), (), s32[]{:S(2)}) async-start(), calls=%async_computation.6 | async-start | bytes 786432 | tf_op jit(solution)/shard_map/psum | solution.py:137
  297.6 7.6 %copy-start.1 = (bf16[32,512,128]{1,0,2:T(8,128)(2,1)S(1)}, bf16[32,512,128]{1,0,2:T(8,128)(2,1)}, u32[]{:S(2)}) copy-start(bf16[32,512,128]{1,0,2:T(8,128)(2,1)} %copy.32) | copy-start | bytes 12582916
  308.6 86.5 %copy-start.13 = (f32[32,32]{1,0:T(8,128)S(1)}, f32[32,32]{1,0:T(8,128)}, u32[]{:S(2)}) copy-start(f32[32,32]{1,0:T(8,128)} %copy-done.12) | copy-start | bytes 12292
  310.6 86.3 %copy-start.6 = (f32[32,32,128]{2,1,0:T(8,128)S(1)}, f32[32,32,128]{2,1,0:T(8,128)}, u32[]{:S(2)}) copy-start(f32[32,32,128]{2,1,0:T(8,128)} %fusion.40) | copy-start | bytes 1572868
  392.4 2.6 copy-start.15
  392.4 2.6 copy-start.20
  393.9 0.8 copy-start.8
  393.9 1.0 copy-start.9
  393.9 1.1 copy-start.10
  393.9 3.0 copy-start.7
  393.9 3.0 copy-start.16
  393.9 3.0 copy-start.21
  395.0 4.7 copy-start.22
Sparse Core Ops, SparseCore 0:
  14.3 86.6 all-gather.2
  126.7 97.0 reduce-scatter.2
  234.6 40.4 all-gather.4
  297.5 94.8 reduce-scatter.4
  474.4 244.8 all-reduce.3
where the time goes:
time: 732 us; the launch traced here: 730 us
  waiting for transfers between devices  549 us (75%)
  blocking collectives  74.5 us (10%)
  local copies, waits for them, and re-layouts  44.6 us (6%)
  matrix products  36.3 us (5%)
  between operations  14.1 us (2%)
  other arithmetic  12 us (2%)
    psum x1, waiting for transfers between devices, on_device(): lax.psum((grad_w_in, grad_w_gate, grad_w_out, grad_gain_in, output_norm_g...  244 us
    reduce_scatter x1, waiting for transfers between devices, on_device(): lax.psum_scatter(jnp.einsum('kih,kjh->ijh', left_rows, right, preferred_e...  97.2 us
    all_gather x1, waiting for transfers between devices, on_device(): left_rows = lax.all_gather(left, 'col', axis=1, tiled=True)  85.2 us
    reduce_scatter x1, waiting for transfers between devices, on_device(): lax.psum_scatter(jnp.einsum('qjh,kjh->qkh', dproduct_all, right, preferre...  81.8 us
    psum x1, blocking collectives, on_device(): lax.psum((grad_w_in, grad_w_gate, grad_w_out, grad_gain_in, output_norm_g...  74.5 us
    all_gather x1, waiting for transfers between devices, on_device(): dproduct_all = lax.all_gather(product_gradient, 'row', axis=0, tiled=True)  40.6 us
  transfers between devices with their start and end apart: 5, of which 5 were waited for; matrix products, arithmetic and copies ran while one was open for 2% of the time, Pallas kernels for 0%

commit v1 on v0

v1 whole, which is shorter than its diff:
```python
import jax
import jax.numpy as jnp
from jax import lax
from jax.experimental import pallas as pl
from jax.experimental.pallas import tpu as pltpu
from jax.sharding import PartitionSpec as P


BLOCK = 128
EPS = 1e-05
F32 = jnp.float32
BF16 = jnp.bfloat16
AXES = ("row", "col")
VMEM_LIMIT = 48 * 1024 * 1024


def dot(x, y, dims):
    return lax.dot_general(x, y, (dims, ((), ())), preferred_element_type=F32)


NN = ((1,), (0,))
NT = ((1,), (1,))
TN = ((0,), (0,))


def norm_rows(values, axis):
    centred = values - jnp.mean(values, axis=axis, keepdims=True)
    rstd = lax.rsqrt(jnp.mean(centred * centred, axis=axis, keepdims=True) + EPS)
    return centred * rstd, rstd


def norm_back(e, nhat, rstd, axis):
    first = jnp.mean(e, axis=axis, keepdims=True)
    second = jnp.mean(e * nhat, axis=axis, keepdims=True)
    return rstd * (e - first - nhat * second)


def swap_segments(v):
    lane = lax.broadcasted_iota(jnp.int32, v[0].shape, 1)
    low = lane < 64
    even = (lane // 32) % 2 == 0
    w = [None] * 4
    for m in range(2):
        w[m] = jnp.where(low, v[m], pltpu.roll(v[m + 2], 64, 1))
        w[m + 2] = jnp.where(low, pltpu.roll(v[m], 64, 1), v[m + 2])
    u = [None] * 4
    for m in (0, 2):
        u[m] = jnp.where(even, w[m], pltpu.roll(w[m + 1], 32, 1))
        u[m + 1] = jnp.where(even, pltpu.roll(w[m], 96, 1), w[m + 1])
    return u


def group(ref, t):
    return ref[:, t].reshape(128, 128)


def project_kernel(pair, mask, gain, w_t, chunks, zn_out, scratch):
    for s in range(2):
        for half in range(4):
            t = 4 * s + half
            nhat, _ = norm_rows(group(pair, t).astype(F32), 1)
            zn = (nhat * gain[...]).astype(BF16)
            zn_out[t] = zn
            proj = dot(w_t[...], zn, NT)
            weight = mask[t : t + 1, :]
            scratch[:, half, :] = jax.nn.sigmoid(proj[128:256]) * proj[:128] * weight
            scratch[:, 4 + half, :] = jax.nn.sigmoid(proj[384:]) * proj[256:384] * weight
        chunks[:, s] = scratch[...].astype(BF16)


def product_kernel(got, x_out, left_out, right_out, rows_a, rows_b):
    sub = lax.broadcasted_iota(jnp.int32, (16, 8, 128), 1) < 4
    for hi in range(4):
        u = swap_segments([got[:, hi, lo].astype(F32).reshape(128, 128) for lo in range(4)])
        for m in range(4):
            block = u[m].reshape(16, 8, 128)
            swapped = jnp.concatenate([block[:, 4:], block[:, :4]], axis=1)
            rows, lanes = pl.ds(128 * m, 128), pl.ds(128 * hi, 128)
            rows_a[rows, lanes] = jnp.where(sub, block, 0.0).reshape(128, 128).astype(BF16)
            right_out[rows, lanes] = jnp.where(sub, swapped, 0.0).reshape(128, 128).astype(BF16)
            left_out[rows, lanes] = jnp.where(sub, 0.0, swapped).reshape(128, 128).astype(BF16)
    x = dot(rows_a[...], right_out[...], TN)
    rows_b[...] = x.reshape(16, 4, 8, 512)
    for hi in range(4):
        lanes = pl.ds(128 * hi, 128)
        u = swap_segments([rows_b[:, m, :, lanes].reshape(128, 128) for m in range(4)])
        for lo in range(4):
            x_out[:, hi, lo] = u[lo].reshape(16, 8, 128).astype(BF16)


def output_kernel(got, zn_in, cot, w_gate, w_out, gain, update, dx_out, dzn, grads, gain_sum, x_all, dx_all):
    x_all[...] = got[:, 0].astype(F32) + got[:, 1].astype(F32)
    for t in range(8):
        xhat, xrstd = norm_rows(x_all[:, t, :], 0)
        xn = (xhat * gain[...]).astype(BF16)
        outp = dot(xn, w_out[...], TN)
        zn = zn_in[t]
        gate = jax.nn.sigmoid(dot(zn, w_gate[...], NN))
        update[:, t] = (gate * outp).astype(BF16).reshape(4, 32, 128)
        dy = group(cot, t).astype(F32)
        dout = (dy * gate).astype(BF16)
        dgpre = (dy * outp * gate * (1.0 - gate)).astype(BF16)
        part_out = dot(xn, dout, NN)
        part_gate = dot(zn, dgpre, TN)
        dxn = dot(w_out[...], dout, NT)
        part_gain = dxn * xhat
        dx_all[:, t, :] = norm_back(dxn * gain[...], xhat, xrstd, 0)
        dzn[t] = dot(dgpre, w_gate[...], NT)
        if t == 0:
            grads[0:128] = part_out
            grads[128:256] = part_gate
            gain_sum[...] = part_gain
        else:
            grads[0:128] += part_out
            grads[128:256] += part_gate
            gain_sum[...] += part_gain
    dx = dx_all[...].astype(BF16)
    dx_out[:, 0] = dx
    dx_out[:, 1] = dx


def back_product_kernel(got, left, right, out, dx_rows, d_rows):
    for hi in range(4):
        u = swap_segments([got[:, hi, lo].astype(F32).reshape(128, 128) for lo in range(4)])
        for m in range(4):
            dx_rows[:, m, :, pl.ds(128 * hi, 128)] = u[m].reshape(16, 8, 128)
    dx = dx_rows[...].reshape(512, 512).astype(BF16)
    d_rows[...] = dot(right[...], dx, NT) + dot(left[...], dx, NN)
    for hi in range(4):
        lanes = pl.ds(128 * hi, 128)
        u = swap_segments([d_rows[pl.ds(128 * m, 128), lanes] for m in range(4)])
        for lo in range(4):
            out[:, hi, lo] = u[lo].reshape(16, 8, 128).astype(BF16)


def input_kernel(got, pair, mask, gain, w_t, dzn_in, grad_pair, grads, gain_sum, d_all):
    for s in range(2):
        d_all[...] = got[:, s].astype(F32)
        for half in range(4):
            t = 4 * s + half
            nhat, rstd = norm_rows(group(pair, t).astype(F32), 1)
            zn = (nhat * gain[...]).astype(BF16)
            proj = dot(w_t[...], zn, NT)
            weight = mask[t : t + 1, :]
            fa = d_all[:, half, :] * weight
            fb = d_all[:, 4 + half, :] * weight
            sa = jax.nn.sigmoid(proj[128:256])
            sb = jax.nn.sigmoid(proj[384:])
            da, db = fa * sa, fb * sb
            dproj = jnp.concatenate(
                [da, da * proj[:128] * (1.0 - sa), db, db * proj[256:384] * (1.0 - sb)], axis=0
            ).astype(BF16)
            part = dot(dproj, zn, NN)
            dzn = dot(dproj, w_t[...], TN) + dzn_in[t]
            part_gain = dzn * nhat
            grad_pair[:, t] = norm_back(dzn * gain[...], nhat, rstd, 1).reshape(4, 32, 128)
            if t == 0:
                grads[...] = part
                gain_sum[...] = part_gain
            else:
                grads[...] += part
                gain_sum[...] += part_gain


def call(kernel, outs, scratch, flops):
    return pl.pallas_call(
        kernel,
        out_shape=[jax.ShapeDtypeStruct(shape, dtype) for shape, dtype in outs],
        scratch_shapes=[pltpu.VMEM(shape, dtype) for shape, dtype in scratch],
        compiler_params=pltpu.CompilerParams(vmem_limit_bytes=VMEM_LIMIT),
        cost_estimate=pl.CostEstimate(flops=flops, bytes_accessed=2000000, transcendentals=0),
    )


def exchange(chunks):
    shape = chunks.shape
    flat = chunks.reshape((256,) + shape[-2:])
    return lax.all_to_all(flat, AXES, 0, 0, tiled=True)


def on_device(pair, cotangent, contact, chain, gain_in, output_norm_gain, w_in, w_gate, w_out):
    row_start = lax.axis_index("row") * 32
    col_start = lax.axis_index("col") * 32
    chain_row = lax.dynamic_slice_in_dim(chain, row_start, 32).reshape(4, 8).T
    chain_col = lax.dynamic_slice_in_dim(chain, col_start, 32)
    listed = contact[col_start // BLOCK, row_start // BLOCK] == 1
    mask = (listed | (chain_row[:, :, None] == chain_col[None, None, :])).astype(F32).reshape(8, 128)
    pair4 = pair.reshape(4, 8, 32, 128)
    cot4 = cotangent.reshape(4, 8, 32, 128)
    gain_row = gain_in.reshape(1, 128)
    gain_col = jnp.broadcast_to(output_norm_gain[:, None], (128, 128))
    w_t = w_in.T

    chunks, zn = call(
        project_kernel,
        [((128, 2, 8, 128), BF16), ((8, 128, 128), BF16)],
        [((128, 8, 128), F32)],
        134217728,
    )(pair4, mask, gain_row, w_t)
    got = exchange(chunks).reshape(16, 4, 4, 8, 128)
    x_chunks, left, right = call(
        product_kernel,
        [((16, 4, 4, 8, 128), BF16), ((512, 512), BF16), ((512, 512), BF16)],
        [((512, 512), BF16), ((16, 4, 8, 512), F32)],
        268435456,
    )(got)
    got = exchange(x_chunks).reshape(128, 2, 8, 128)
    update, dx_chunks, dzn, grads_early, gain_part = call(
        output_kernel,
        [
            ((4, 8, 32, 128), BF16),
            ((128, 2, 8, 128), BF16),
            ((8, 128, 128), F32),
            ((256, 128), F32),
            ((128, 128), F32),
        ],
        [((128, 8, 128), F32), ((128, 8, 128), F32)],
        201326592,
    )(got, zn, cot4, w_gate, w_out, gain_col)
    got = exchange(dx_chunks).reshape(16, 4, 4, 8, 128)
    (d_chunks,) = call(
        back_product_kernel,
        [((16, 4, 4, 8, 128), BF16)],
        [((16, 4, 8, 512), F32), ((512, 512), F32)],
        536870912,
    )(got, left, right)
    got = exchange(d_chunks).reshape(128, 2, 8, 128)
    grad_pair, grads_late, gain_in_part = call(
        input_kernel,
        [((4, 8, 32, 128), F32), ((512, 128), F32), ((128, 128), F32)],
        [((128, 8, 128), F32)],
        402653184,
    )(got, pair4, mask, gain_row, w_t, dzn)

    gains = jnp.zeros((256, 128), F32)
    gains = gains.at[0].set(jnp.sum(gain_in_part, axis=0)).at[1].set(jnp.sum(gain_part, axis=1))
    parts = jnp.stack([grads_late[:256], grads_late[256:], grads_early, gains], axis=1)
    parts = lax.all_to_all(parts.astype(BF16), AXES, 0, 0, tiled=True)
    total = jnp.sum(parts.astype(F32), axis=0)
    total = jnp.broadcast_to(total.astype(BF16)[None], (256, 4, 128))
    total = lax.all_to_all(total, AXES, 0, 0, tiled=True).astype(F32)
    grad_w_in = jnp.concatenate([total[:, 0], total[:, 1]], axis=0).T
    return (
        update.reshape(32, 32, 128),
        grad_pair.reshape(32, 32, 128),
        grad_w_in,
        total[128:, 2],
        total[:128, 2],
        total[0, 3],
        total[1, 3],
    )


def solution(mesh):
    return jax.shard_map(
        on_device,
        mesh=mesh,
        in_specs=(P("row", "col", None), P("row", "col", None), P(), P(), P(), P(), P(), P(), P()),
        out_specs=(P("row", "col", None), P("row", "col", None), P(), P(), P(), P(), P()),
        check_vma=False,
    )
```

time: 732 us -> 178 us (0.24)
  waiting for transfers between devices: 549 us -> 20.7 us
  blocking collectives: 74.5 us -> 131 us
  local copies, waits for them, and re-layouts: 44.6 us -> 7.37 us
  matrix products: 36.3 us -> 0 us
  between operations: 14.1 us -> 1.48 us
  other arithmetic: 12 us -> 0.57 us
  Pallas kernels: 0 us -> 11.1 us
    psum x1 -> x0, waiting for transfers between devices: 244 us -> none  [on_device(): lax.psum((grad_w_in, grad_w_gate, grad_w_out, grad_gain_in, output_norm_g...]
    reduce_scatter x2 -> x0, waiting for transfers between devices: 179 us -> none  [the longest x1 97.2 us: on_device(): lax.psum_scatter(jnp.einsum('kih,kjh->ijh', left_rows, right, preferred_e...]
    all_to_all x0 -> x5, blocking collectives: none -> 131 us  [the longest x3 88.7 us: exchange(): return lax.all_to_all(flat, AXES, 0, 0, tiled=True)]
    all_gather x2 -> x0, waiting for transfers between devices: 126 us -> none  [the longest x1 85.2 us: on_device(): left_rows = lax.all_gather(left, 'col', axis=1, tiled=True)]
    psum x1 -> x0, blocking collectives: 74.5 us -> none  [on_device(): lax.psum((grad_w_in, grad_w_gate, grad_w_out, grad_gain_in, output_norm_g...]
    dot_general x14 -> x0, matrix products: 36.3 us -> none  [the longest x1 6.69 us: on_device(): jnp.einsum('kih,kjh->ijh', left_rows, right, preferred_element_type=jnp.f...]
    all_to_all x0 -> x1, waiting for transfers between devices: none -> 20.7 us  [exchange(): return lax.all_to_all(flat, AXES, 0, 0, tiled=True)]
    all_gather x2 -> x0, local copies, waits for them, and re-layouts: 16.5 us -> none  [the longest x1 8.64 us: on_device(): dproduct_all = lax.all_gather(product_gradient, 'row', axis=0, tiled=True)]
  transfers between devices with their start and end apart: 5 -> 1, of which waited for: 5 -> 1; matrix products, arithmetic and copies ran while one was open for 2% -> 0% of each run, Pallas kernels for 0% -> 0%
where the time goes in v1:
time: 178 us; the launch traced here: 177 us
  blocking collectives  131 us (74%)
  waiting for transfers between devices  20.7 us (12%)
  Pallas kernels  11.1 us (6%)
  local copies, waits for them, and re-layouts  7.37 us (4%)
  starting transfers between devices  5.48 us (3%)
    all_to_all x3, blocking collectives, exchange(): return lax.all_to_all(flat, AXES, 0, 0, tiled=True)  88.7 us
    all_to_all x1, blocking collectives, on_device(): parts = lax.all_to_all(parts.astype(BF16), AXES, 0, 0, tiled=True)  21 us
    all_to_all x1, blocking collectives, on_device(): total = lax.all_to_all(total, AXES, 0, 0, tiled=True).astype(F32)  20.9 us
    all_to_all x1, waiting for transfers between devices, exchange(): return lax.all_to_all(flat, AXES, 0, 0, tiled=True)  20.7 us
    all_to_all x1, starting transfers between devices, exchange(): return lax.all_to_all(flat, AXES, 0, 0, tiled=True)  5.48 us
  transfers between devices with their start and end apart: 1, of which 1 were waited for; matrix products, arithmetic and copies ran while one was open for 0% of the time, Pallas kernels for 0%

profile of v1, /device:TPU:1, one launch (start us, length us, event | category | flops | bytes accessed | tf_op | source)
XLA Modules:
  0.0 177.3 jit_solution(9065968124558536857)
XLA Ops:
  0.7 0.8 fusion.2
  1.5 0.1 eq.31
  1.6 0.1 reshape.119
  1.7 0.1 copy.20
  1.8 0.1 eq.28
  1.9 0.1 eq.29
  1.9 0.1 copy.21
  2.1 1.3 dynamic_slice.9
  4.0 0.6 copy-done.4
  4.7 1.3 shard_map.144
  6.0 36.4 %all_to_all.30 = bf16[256,8,128]{2,1,0:T(8,128)(2,1)S(1)} all-to-all(bf16[256,8,128]{2,1,0:T(8,128)(2,1)S(1)} %bitcast.46), channel_id=1, replica_groups=mesh['row'=16,'col'=16] {'row','col'}, dimensions={0} | all-to-all | bytes 1048576 | tf_op jit(solution)/shard_map/all_to_all | solution.py:178
  42.4 1.4 shard_map.145
  43.8 26.2 %all_to_all.31 = bf16[256,8,128]{2,1,0:T(8,128)(2,1)S(1)} all-to-all(bf16[256,8,128]{2,1,0:T(8,128)(2,1)S(1)} %bitcast.45), channel_id=1, replica_groups=mesh['row'=16,'col'=16] {'row','col'}, dimensions={0} | all-to-all | bytes 1048576 | tf_op jit(solution)/shard_map/all_to_all | solution.py:178
  70.0 0.7 copy-done.6
  70.6 0.1 broadcast_in_dim.4.gain
  70.7 0.7 copy-done.1
  71.4 2.9 %shard_map.146 = (bf16[4,8,32,128]{3,2,1,0:T(8,128)(2,1)}, bf16[128,2,8,128]{3,2,1,0:T(8,128)(2,1)S(1)}, f32[8,128,128]{2,1,0:T(8,128)S(1)}, f32[256,128]{1,0:T(8,128)S(1)}, f32[128,128]{1,0:T(8,128)S(1)}) custom-call(bf16[128,2,8,128]{3,2,1,0:T(8,128)(2,1)S(1)} %bitcast.40, bf16[8,128,128]{2,1,0:T(8,128)(2,1)S(1)} %get-tuple-element.46.zn_in, ...), custom_call_target="tpu_custom_call" | custom-call | flops 201326592 | bytes 2000000 | tf_op jit(solution)/shard_map/pallas_call | solution.py:208
  74.3 26.1 %all_to_all.32 = bf16[256,8,128]{2,1,0:T(8,128)(2,1)S(1)} all-to-all(bf16[256,8,128]{2,1,0:T(8,128)(2,1)S(1)} %bitcast.43), channel_id=1, replica_groups=mesh['row'=16,'col'=16] {'row','col'}, dimensions={0} | all-to-all | bytes 1048576 | tf_op jit(solution)/shard_map/all_to_all | solution.py:178
  100.4 2.1 %shard_map.147 = bf16[16,4,4,8,128]{4,3,2,1,0:T(8,128)(2,1)} custom-call(bf16[16,4,4,8,128]{4,3,2,1,0:T(8,128)(2,1)S(1)} %bitcast.41, bf16[512,512]{1,0:T(8,128)(2,1)S(1)} %get-tuple-element.49.left, bf16[512,512]{1,0:T(8,128)(2,1)S(1)} %get-tuple-element.50.right), custom_call_target="tpu_custom_call" | custom-call | flops 536870912 | bytes 2000000 | tf_op jit(solution)/shard_map/pallas_call | solution.py:221
  102.5 5.5 %all-to-all-start.3 = ((bf16[256,8,128]{2,1,0:T(8,128)(2,1)}), bf16[256,8,128]{2,1,0:T(8,128)(2,1)S(1)}, u32[]{:S(2)}, u32[]{:S(2)}) async-start(bf16[256,8,128]{2,1,0:T(8,128)(2,1)} %bitcast.13), calls=%async_computation.3 | async-start | bytes 1048576 | tf_op jit(solution)/shard_map/all_to_all | solution.py:178
  108.0 0.1 reduce_sum.31
  108.1 20.7 %all-to-all-done.3 = bf16[256,8,128]{2,1,0:T(8,128)(2,1)S(1)} async-done(((bf16[256,8,128]{2,1,0:T(8,128)(2,1)}), bf16[256,8,128]{2,1,0:T(8,128)(2,1)S(1)}, u32[]{:S(2)}, u32[]{:S(2)}) %all-to-all-start.3) | async-done | bytes 524320 | tf_op jit(solution)/shard_map/all_to_all | solution.py:178
  128.9 3.4 %shard_map.148 = (f32[4,8,32,128]{3,2,1,0:T(8,128)}, f32[512,128]{1,0:T(8,128)S(1)}, f32[128,128]{1,0:T(8,128)S(1)}) custom-call(bf16[128,2,8,128]{3,2,1,0:T(8,128)(2,1)S(1)} %bitcast.42, bf16[4,8,32,128]{3,2,1,0:T(8,128)(2,1)S(1)} %bitcast.51, f32[8,128]{1,0:T(8,128)S(1)} %or_convert_fusion.mask, f32[1,128]{1,0:T(1,128)S(1)} %bitcast.53, ...), custom_call_target="tpu_custom_call" | custom-call | flops 402653184 | bytes 2000000 | tf_op jit(solution)/shard_map/pallas_call | solution.py:228
  132.4 0.2 copy.23
  132.7 21.0 %all_to_all.33 = bf16[256,4,128]{2,1,0:T(4,128)(2,1)S(1)} all-to-all(bf16[256,4,128]{2,1,0:T(4,128)(2,1)S(1)} %copy.23), channel_id=1, replica_groups=mesh['row'=16,'col'=16] {'row','col'}, dimensions={0} | all-to-all | bytes 524288 | tf_op jit(solution)/shard_map/all_to_all | solution.py:238
  153.6 0.3 reduce_sum.32
  153.9 0.1 broadcast_in_dim.5
  154.0 20.9 %all_to_all.34 = bf16[256,4,128]{2,1,0:T(4,128)(2,1)S(1)} all-to-all(bf16[256,4,128]{2,1,0:T(4,128)(2,1)S(1)} %broadcast_in_dim.5), channel_id=1, replica_groups=mesh['row'=16,'col'=16] {'row','col'}, dimensions={0} | all-to-all | bytes 524288 | tf_op jit(solution)/shard_map/all_to_all | solution.py:241
  174.9 0.2 fusion.1
  175.1 0.8 copy.25
  176.0 0.5 slice_bitcast_fusion.2
  176.5 0.8 fusion
  (22 shorter events, 0.3 us)
Async XLA Ops:
  0.6 1.3 copy-start.5
  0.6 3.4 %copy-start.3 = (bf16[32,32,128]{2,1,0:T(8,128)(2,1)S(1)}, bf16[32,32,128]{2,1,0:T(8,128)(2,1)}, u32[]{:S(2)}) copy-start(bf16[32,32,128]{2,1,0:T(8,128)(2,1)} %param.13) | copy-start | bytes 786436
  4.0 0.7 copy-start.4
  43.8 26.9 %copy-start = (bf16[32,32,128]{2,1,0:T(8,128)(2,1)S(1)}, bf16[32,32,128]{2,1,0:T(8,128)(2,1)}, u32[]{:S(2)}) copy-start(bf16[32,32,128]{2,1,0:T(8,128)(2,1)} %param.14) | copy-start | bytes 786436
  70.0 0.7 copy-start.6
  70.6 0.8 copy-start.1
  70.6 0.8 copy-start.2
  102.5 26.4 %all-to-all-start.3 = ((bf16[256,8,128]{2,1,0:T(8,128)(2,1)}), bf16[256,8,128]{2,1,0:T(8,128)(2,1)S(1)}, u32[]{:S(2)}, u32[]{:S(2)}) async-start(bf16[256,8,128]{2,1,0:T(8,128)(2,1)} %bitcast.13), calls=%async_computation.3 | async-start | bytes 1048576 | tf_op jit(solution)/shard_map/all_to_all | solution.py:178

commit v2 on v1

v2 whole, which is shorter than its diff:
```python
import jax
import jax.numpy as jnp
from jax import lax
from jax.experimental import pallas as pl
from jax.experimental.pallas import tpu as pltpu
from jax.sharding import PartitionSpec as P


BLOCK = 128
EPS = 1e-05
F32 = jnp.float32
BF16 = jnp.bfloat16
AXES = ("row", "col")
VMEM_LIMIT = 48 * 1024 * 1024


def dot(x, y, dims):
    return lax.dot_general(x, y, (dims, ((), ())), preferred_element_type=F32)


NN = ((1,), (0,))
NT = ((1,), (1,))
TN = ((0,), (0,))


def norm_rows(values, axis):
    centred = values - jnp.mean(values, axis=axis, keepdims=True)
    rstd = lax.rsqrt(jnp.mean(centred * centred, axis=axis, keepdims=True) + EPS)
    return centred * rstd, rstd


def norm_back(e, nhat, rstd, axis):
    first = jnp.mean(e, axis=axis, keepdims=True)
    second = jnp.mean(e * nhat, axis=axis, keepdims=True)
    return rstd * (e - first - nhat * second)


def swap_segments(v):
    lane = lax.broadcasted_iota(jnp.int32, v[0].shape, 1)
    low = lane < 64
    even = (lane // 32) % 2 == 0
    w = [None] * 4
    for m in range(2):
        w[m] = jnp.where(low, v[m], pltpu.roll(v[m + 2], 64, 1))
        w[m + 2] = jnp.where(low, pltpu.roll(v[m], 64, 1), v[m + 2])
    u = [None] * 4
    for m in (0, 2):
        u[m] = jnp.where(even, w[m], pltpu.roll(w[m + 1], 32, 1))
        u[m + 1] = jnp.where(even, pltpu.roll(w[m], 96, 1), w[m + 1])
    return u


def group(ref, t):
    return ref[:, t].reshape(128, 128)


def fetch(pairs, sems):
    copies = [pltpu.make_async_copy(far, near, sems.at[n]) for n, (far, near) in enumerate(pairs)]
    for copy in copies:
        copy.start()
    return copies


def project_kernel(contact, chain, pair_far, gain_far, w_far, chunks, zn_out, mask_out, w_t, pair, gain, w_in, left, right, sems):
    copies = fetch([(w_far, w_in), (gain_far, gain), (pair_far, pair)], sems)
    row_start = lax.axis_index("row") * 32
    col_start = lax.axis_index("col") * 32
    lane = lax.broadcasted_iota(jnp.int32, (8, 128), 1)
    sub = lax.broadcasted_iota(jnp.int32, (8, 128), 0)
    col_id = jnp.zeros((8, 128), jnp.int32)
    row_id = jnp.zeros((8, 128), jnp.int32)
    for n in range(32):
        col_id = jnp.where(lane % 32 == n, chain[col_start + n], col_id)
        row_id = jnp.where((sub == n % 8) & (lane // 32 == n // 8), chain[row_start + n], row_id)
    listed = contact[col_start // BLOCK, row_start // BLOCK]
    mask = jnp.where(row_id == col_id, 1.0, jnp.where(listed == 1, 1.0, 0.0))
    mask_out[...] = mask
    for copy in copies:
        copy.wait()
    w_t[...] = w_in[...].astype(F32).T.astype(BF16)
    for t in range(8):
        nhat, _ = norm_rows(group(pair, t).astype(F32), 1)
        zn = (nhat * gain[...]).astype(BF16)
        zn_out[t] = zn
        proj = dot(w_t[...], zn, NT)
        weight = mask[t : t + 1, :]
        left[:, t, :] = jax.nn.sigmoid(proj[128:256]) * proj[:128] * weight
        right[:, t, :] = jax.nn.sigmoid(proj[384:]) * proj[256:384] * weight
    chunks[:, 0] = left[...].astype(BF16)
    chunks[:, 1] = right[...].astype(BF16)


def product_kernel(got, keep, send, left, right, x_all):
    for hi in range(4):
        for ab, rows in enumerate((left, right)):
            u = swap_segments([got[:, hi, lo, ab].astype(F32).reshape(64, 128) for lo in range(4)])
            for m in range(4):
                rows[pl.ds(64 * m, 64), pl.ds(128 * hi, 128)] = u[m].astype(BF16)
    x_all[...] = dot(left[...], right[...], TN).reshape(8, 2, 32, 512)
    core = lax.axis_index("row") % 2
    keep[...] = x_all[:, core]
    send[...] = x_all[:, 1 - core]


def product_sum_kernel(keep, came, x_out):
    for hi in range(4):
        lanes = pl.ds(128 * hi, 128)
        u = swap_segments(
            [(keep[:, pl.ds(8 * m, 8), lanes] + came[:, pl.ds(8 * m, 8), lanes]).reshape(64, 128) for m in range(4)]
        )
        for lo in range(4):
            x_out[:, hi, lo] = u[lo].reshape(8, 8, 128).astype(BF16)


def column_of(row):
    return jnp.broadcast_to(row, (128, 128)).T


def output_kernel(
    got, zn_in, cot_far, gate_far, out_far, gain, update, dx_out, xn_out, dout_out, dgpre_out, x_all, dx_all, cot, w_gate, w_out, sems
):
    copies = fetch([(gate_far, w_gate), (out_far, w_out), (cot_far, cot)], sems)
    gain_col = column_of(gain[...])
    x_all[...] = got[...].astype(F32)
    for copy in copies:
        copy.wait()
    for t in range(8):
        xhat, xrstd = norm_rows(x_all[:, t, :], 0)
        xn = (xhat * gain_col).astype(BF16)
        outp = dot(xn, w_out[...], TN)
        gate = jax.nn.sigmoid(dot(zn_in[t], w_gate[...], NN))
        update[:, t] = (gate * outp).astype(BF16).reshape(4, 32, 128)
        dy = group(cot, t).astype(F32)
        dout = (dy * gate).astype(BF16)
        dxn = dot(w_out[...], dout, NT)
        dx_all[:, t, :] = norm_back(dxn * gain_col, xhat, xrstd, 0)
        xn_out[t] = xn
        dout_out[t] = dout
        dgpre_out[t] = (dy * outp * gate * (1.0 - gate)).astype(BF16)
    dx_out[...] = dx_all[...].astype(BF16)


def output_grads_kernel(xn, dout, dgpre, zn, w_gate, w_out, gain_in, gain, dzn, grads, gains):
    out_sum = jnp.zeros((128, 128), F32)
    gate_sum = jnp.zeros((128, 128), F32)
    for t in range(8):
        out_sum += dot(xn[t], dout[t], NN)
        gate_sum += dot(dgpre[t], zn[t], TN)
        dzn[t] = dot(dgpre[t], w_gate[...], NT)
    grads[:128] = out_sum
    grads[128:] = gate_sum
    column = jnp.sum(out_sum * w_out[...].astype(F32), axis=1, keepdims=True) / column_of(gain[...])
    row = jnp.sum(gate_sum * w_gate[...].astype(F32).T, axis=0, keepdims=True) / gain_in[...]
    first = lax.broadcasted_iota(jnp.int32, (8, 128), 0) == 0
    gains[...] = jnp.where(first, row, column.T[:8])


def back_product_kernel(got, came, left, right, out, dx_rows, d_rows):
    core = lax.axis_index("row") % 2
    for hi in range(4):
        for source, place in ((got, core), (came, 1 - core)):
            u = swap_segments([source[:, hi, lo].astype(F32).reshape(64, 128) for lo in range(4)])
            for m in range(4):
                dx_rows[:, place, m, :, pl.ds(128 * hi, 128)] = u[m].reshape(8, 8, 128)
    dx = dx_rows[...].reshape(512, 512).astype(BF16)
    d_rows[0] = dot(right[...], dx, NT)
    d_rows[1] = dot(left[...], dx, NN)
    for hi in range(4):
        for ab in range(2):
            u = swap_segments([d_rows[ab, pl.ds(64 * m, 64), pl.ds(128 * hi, 128)] for m in range(4)])
            for lo in range(4):
                out[:, hi, lo, ab] = u[lo].reshape(8, 8, 128).astype(BF16)


def input_grads_kernel(got, zn_in, mask, gain, w_t, early, early_gains, dproj_out, grads, d_left, d_right):
    total = jnp.zeros((512, 128), F32)
    d_left[...] = got[:, 0].astype(F32)
    d_right[...] = got[:, 1].astype(F32)
    for t in range(8):
        zn = zn_in[t]
        proj = dot(w_t[...], zn, NT)
        weight = mask[t : t + 1, :]
        sa = jax.nn.sigmoid(proj[128:256])
        sb = jax.nn.sigmoid(proj[384:])
        da = d_left[:, t, :] * weight * sa
        db = d_right[:, t, :] * weight * sb
        dproj = jnp.concatenate(
            [da, da * proj[:128] * (1.0 - sa), db, db * proj[256:384] * (1.0 - sb)], axis=0
        ).astype(BF16)
        dproj_out[t] = dproj
        total += dot(dproj, zn, NN)
    row = jnp.sum(total * w_t[...].astype(F32), axis=0, keepdims=True) / gain[...]
    first = lax.broadcasted_iota(jnp.int32, (8, 128), 0) == 0
    gains = early_gains[...] + jnp.where(first, row, 0.0)
    grads[...] = jnp.concatenate(
        [
            total.reshape(32, 16, 128),
            early[...].reshape(32, 8, 128),
            jnp.broadcast_to(gains[None], (32, 8, 128)),
        ],
        axis=1,
    ).astype(BF16)


def input_kernel(dproj, pair, gain, w_t, dzn_in, grad_pair):
    for t in range(8):
        nhat, rstd = norm_rows(group(pair, t).astype(F32), 1)
        dzn = dot(dproj[t], w_t[...], TN) + dzn_in[t]
        grad_pair[:, t] = norm_back(dzn * gain[...], nhat, rstd, 1).reshape(4, 32, 128)


def sum_kernel(parts, out):
    total = jnp.sum(parts[...].astype(F32), axis=0, keepdims=True)
    out[...] = jnp.broadcast_to(total, out.shape).astype(BF16)


def unpack_kernel(got, grad_in, grad_gate, grad_out, grad_gain, grad_out_gain):
    total = got[...].astype(F32)
    grad_in[...] = total[:, :16].reshape(512, 128).T
    early = total[:, 16:24].reshape(256, 128)
    grad_out[...] = early[:128]
    grad_gate[...] = early[128:].T
    grad_gain[...] = total[0, 24:25]
    grad_out_gain[...] = total[0, 25:26]


VMEM = pl.BlockSpec(memory_space=pltpu.VMEM)
SMEM = pl.BlockSpec(memory_space=pltpu.SMEM)
FAR = pl.BlockSpec(memory_space=pltpu.HBM)


def call(kernel, outs, scratch, flops, specs):
    return pl.pallas_call(
        kernel,
        out_shape=[jax.ShapeDtypeStruct(shape, dtype) for shape, dtype in outs],
        in_specs=specs,
        scratch_shapes=scratch,
        compiler_params=pltpu.CompilerParams(vmem_limit_bytes=VMEM_LIMIT),
        cost_estimate=pl.CostEstimate(flops=flops, bytes_accessed=2000000, transcendentals=0),
    )


def groups_by(place):
    found = {}
    for device in range(256):
        group_id, order = place(device // 16, device % 16)
        found.setdefault(group_id, []).append((order, device))
    return [[device for _, device in sorted(members)] for _, members in sorted(found.items())]


SAME_CORE = groups_by(lambda row, col: (row % 2, (row // 2, col)))
PLANE = groups_by(lambda row, col: ((col // 4, row // 2 % 2), (row // 4, row % 2, col % 4)))
LINE = groups_by(lambda row, col: ((row // 4, row % 2, col % 4), (col // 4, row // 2 % 2)))


def exchange(chunks, groups):
    return lax.all_to_all(chunks, AXES, 0, 0, tiled=True, axis_index_groups=groups)


def swap_cores(array):
    return lax.ppermute(array, "row", [(row, row ^ 1) for row in range(16)])


def sum_parts(parts, copies):
    (out,) = call(sum_kernel, [((copies, 32, 128), BF16)], [], 1000000, [VMEM])(parts)
    return out


def on_device(pair, cotangent, contact, chain, gain_in, output_norm_gain, w_in, w_gate, w_out):
    pair4 = pair.reshape(4, 8, 32, 128)
    cot4 = cotangent.reshape(4, 8, 32, 128)
    gain_row = gain_in.reshape(1, 128)
    out_gain_row = output_norm_gain.reshape(1, 128)
    flat = ((8, 128, 128), BF16)
    tiles = pltpu.VMEM((128, 8, 128), F32)

    chunks, zn, mask, w_t = call(
        project_kernel,
        [((128, 2, 8, 128), BF16), flat, ((8, 128), F32), ((512, 128), BF16)],
        [
            pltpu.VMEM((4, 8, 32, 128), BF16),
            pltpu.VMEM((1, 128), F32),
            pltpu.VMEM((128, 512), BF16),
            tiles,
            tiles,
            pltpu.SemaphoreType.DMA((3,)),
        ],
        134217728,
        [SMEM, SMEM, FAR, FAR, FAR],
    )(contact, chain, pair4, gain_row, w_in)
    got = exchange(chunks, SAME_CORE).reshape(8, 4, 4, 2, 8, 128)
    rows = ((256, 512), BF16)
    keep, send, left, right = call(
        product_kernel,
        [((8, 32, 512), F32), ((8, 32, 512), F32), rows, rows],
        [pltpu.VMEM((8, 2, 32, 512), F32)],
        134217728,
        [VMEM],
    )(got)
    (x_chunks,) = call(product_sum_kernel, [((8, 4, 4, 8, 128), BF16)], [], 1000000, [VMEM] * 2)(keep, swap_cores(send))
    got = exchange(x_chunks.reshape(128, 8, 128), SAME_CORE)
    update, dx_chunks, xn, dout, dgpre = call(
        output_kernel,
        [((4, 8, 32, 128), BF16), ((128, 8, 128), BF16), flat, flat, flat],
        [
            tiles,
            tiles,
            pltpu.VMEM((4, 8, 32, 128), BF16),
            pltpu.VMEM((128, 128), BF16),
            pltpu.VMEM((128, 128), BF16),
            pltpu.SemaphoreType.DMA((3,)),
        ],
        100663296,
        [VMEM, VMEM, FAR, FAR, FAR, VMEM],
    )(got, zn, cot4, w_gate, w_out, out_gain_row)
    got = exchange(dx_chunks, SAME_CORE)
    dzn, early, early_gains = call(
        output_grads_kernel,
        [((8, 128, 128), F32), ((256, 128), F32), ((8, 128), F32)],
        [],
        100663296,
        [VMEM] * 8,
    )(xn, dout, dgpre, zn, w_gate, w_out, gain_row, out_gain_row)
    came = swap_cores(got)
    blocks = (8, 4, 4, 8, 128)
    (d_chunks,) = call(
        back_product_kernel,
        [((8, 4, 4, 2, 8, 128), BF16)],
        [pltpu.VMEM((8, 2, 4, 8, 512), F32), pltpu.VMEM((2, 256, 512), F32)],
        268435456,
        [VMEM] * 4,
    )(got.reshape(blocks), came.reshape(blocks), left, right)
    got = exchange(d_chunks.reshape(128, 2, 8, 128), SAME_CORE)
    dproj, parts = call(
        input_grads_kernel,
        [((8, 512, 128), BF16), ((32, 32, 128), BF16)],
        [tiles, tiles],
        268435456,
        [VMEM] * 7,
    )(got, zn, mask, gain_row, w_t, early, early_gains)
    parts = exchange(parts, PLANE)
    (grad_pair,) = call(input_kernel, [((4, 8, 32, 128), F32)], [], 134217728, [VMEM] * 5)(dproj, pair4, gain_row, w_t, dzn)
    parts = exchange(sum_parts(parts, 8), LINE)
    parts = exchange(sum_parts(parts, 32), PLANE)
    grad_w_in, grad_w_gate, grad_w_out, grad_gain, grad_out_gain = call(
        unpack_kernel,
        [((128, 512), F32), ((128, 128), F32), ((128, 128), F32), ((1, 128), F32), ((1, 128), F32)],
        [],
        1000000,
        [VMEM],
    )(parts)
    return (
        update.reshape(32, 32, 128),
        grad_pair.reshape(32, 32, 128),
        grad_w_in,
        grad_w_gate,
        grad_w_out,
        grad_gain.reshape(128),
        grad_out_gain.reshape(128),
    )


def solution(mesh):
    return jax.shard_map(
        on_device,
        mesh=mesh,
        in_specs=(P("row", "col", None), P("row", "col", None), P(), P(), P(), P(), P(), P(), P()),
        out_specs=(P("row", "col", None), P("row", "col", None), P(), P(), P(), P(), P()),
        check_vma=False,
    )
```

time: 178 us -> 161 us (0.904)
  blocking collectives: 131 us -> 96 us
  starting transfers between devices: 5.48 us -> 18.4 us
  waiting for transfers between devices: 20.7 us -> 27.7 us
  local copies, waits for them, and re-layouts: 7.37 us -> 3.87 us
  Pallas kernels: 11.1 us -> 13.4 us
    all_to_all x5, blocking collectives: 131 us -> 96 us  [exchange(): lax.all_to_all(chunks, AXES, 0, 0, tiled=True, axis_index_groups=groups)]
    all_to_all x1 -> x2, starting transfers between devices: 5.48 us -> 12 us  [exchange(): lax.all_to_all(chunks, AXES, 0, 0, tiled=True, axis_index_groups=groups)]
    ppermute x0 -> x2, starting transfers between devices: none -> 6.36 us  [swap_cores(): return lax.ppermute(array, 'row', [(row, row ^ 1) for row in range(16)])]
    all_to_all x1 -> x2, waiting for transfers between devices: 20.7 us -> 25 us  [exchange(): lax.all_to_all(chunks, AXES, 0, 0, tiled=True, axis_index_groups=groups)]
    ppermute x0 -> x2, waiting for transfers between devices: none -> 2.7 us  [swap_cores(): return lax.ppermute(array, 'row', [(row, row ^ 1) for row in range(16)])]
    pallas_call x5 -> x11, Pallas kernels: 11.1 us -> 13.4 us  [the longest x1 2.48 us: on_device(): call(input_kernel, [((4, 8, 32, 128), F32)], [], 134217728, [VMEM] * 5)]
    dynamic_slice x2 -> x0, local copies, waits for them, and re-layouts: 2.11 us -> none  [the longest x1 1.27 us: on_device(): listed = contact[col_start // BLOCK, row_start // BLOCK] == 1]
    unnamed x16 -> x20, local copies, waits for them, and re-layouts: 2.96 us -> 3.87 us
  transfers between devices with their start and end apart: 1 -> 4, of which waited for: 1 -> 4; matrix products, arithmetic and copies ran while one was open for 0% -> 0% of each run, Pallas kernels for 0% -> 2%
where the time goes in v2:
time: 161 us; the launch traced here: 160 us
  blocking collectives  96 us (60%)
  waiting for transfers between devices  27.7 us (17%)
  starting transfers between devices  18.4 us (11%)
  Pallas kernels  13.4 us (8%)
  local copies, waits for them, and re-layouts  3.87 us (2%)
    all_to_all x5, blocking collectives, exchange(): lax.all_to_all(chunks, AXES, 0, 0, tiled=True, axis_index_groups=groups)  96 us
    all_to_all x2, waiting for transfers between devices, exchange(): lax.all_to_all(chunks, AXES, 0, 0, tiled=True, axis_index_groups=groups)  25 us
    all_to_all x2, starting transfers between devices, exchange(): lax.all_to_all(chunks, AXES, 0, 0, tiled=True, axis_index_groups=groups)  12 us
    ppermute x2, starting transfers between devices, swap_cores(): return lax.ppermute(array, 'row', [(row, row ^ 1) for row in range(16)])  6.36 us
    unnamed x20, local copies, waits for them, and re-layouts  3.87 us
  transfers between devices with their start and end apart: 4, of which 4 were waited for; matrix products, arithmetic and copies ran while one was open for 0% of the time, Pallas kernels for 2%

profile of v2, /device:TPU:1, one launch (start us, length us, event | category | flops | bytes accessed | tf_op | source)
XLA Modules:
  0.0 160.1 jit_solution(18428351380148502444)
XLA Ops:
  0.7 0.7 copy-done.8
  1.3 0.0 copy-done.5
  1.3 0.9 copy-done.1
  2.3 0.9 copy-done.7
  3.2 0.7 copy-done.9
  3.9 2.4 %shard_map.144 = (bf16[128,2,8,128]{3,2,1,0:T(8,128)(2,1)S(1)}, bf16[8,128,128]{2,1,0:T(8,128)(2,1)S(1)}, f32[8,128]{1,0:T(8,128)S(1)}, bf16[512,128]{1,0:T(8,128)(2,1)S(1)}) custom-call(s32[4,4]{1,0:T(4,128)S(1)} %copy-done.8, s32[512]{0:T(512)S(1)} %copy-done.9, bf16[4,8,32,128]{3,2,1,0:T(8,128)(2,1)S(1)} %bitcast.18, f32[1,128]{1,0:T(1,128)S(1)} %bitcast.20, ...), custom_call_target="tpu_custom_call" | custom-call | flops 134217728 | bytes 2000000 | tf_op jit(solution)/shard_map/pallas_call | solution.py:277
  6.2 34.4 %all_to_all.35 = bf16[128,2,8,128]{3,2,1,0:T(8,128)(2,1)S(1)} all-to-all(bf16[128,2,8,128]{3,2,1,0:T(8,128)(2,1)S(1)} %get-tuple-element.30), channel_id=1, replica_groups={{0,1,2,3,4,5,6,7,8,9,10,11,12,13,14,15,32,33,34,35,36,37,38,39,40,41,42..., dimensions={0} | all-to-all | bytes 1048576 | tf_op jit(solution)/shard_map/all_to_all | solution.py:257
  40.6 1.0 shard_map.145
  41.6 3.1 %collective-permute-start = (f32[8,32,512]{2,1,0:T(8,128)S(1)}, f32[8,32,512]{2,1,0:T(8,128)S(1)}, u32[]{:S(2)}, u32[]{:S(2)}) collective-permute-start(f32[8,32,512]{2,1,0:T(8,128)S(1)} %get-tuple-element.32), channel_id=1, source_target_pairs={{0,16},{16,0},{32,48},{48,32},{64,80},{80,64},{96,112},{112,96},{1... | collective-permute-start | bytes 1572872 | tf_op jit(solution)/shard_map/ppermute | solution.py:261
  44.7 1.5 collective-permute-done.came
  46.2 0.4 shard_map.146
  46.6 0.0 copy-start
  46.6 0.0 copy-start.3
  46.6 0.0 copy-start.4
  46.6 19.0 %all_to_all.36.got = bf16[128,8,128]{2,1,0:T(8,128)(2,1)S(1)} all-to-all(bf16[128,8,128]{2,1,0:T(8,128)(2,1)S(1)} %bitcast.14), channel_id=1, replica_groups={{0,1,2,3,4,5,6,7,8,9,10,11,12,13,14,15,32,33,34,35,36,37,38,39,40,41,42..., dimensions={0} | all-to-all | bytes 524288 | tf_op jit(solution)/shard_map/all_to_all | solution.py:257
  65.7 0.6 copy-done.6
  66.3 1.7 %shard_map.147 = (bf16[4,8,32,128]{3,2,1,0:T(8,128)(2,1)}, bf16[128,8,128]{2,1,0:T(8,128)(2,1)S(1)}, bf16[8,128,128]{2,1,0:T(8,128)(2,1)S(1)}, bf16[8,128,128]{2,1,0:T(8,128)(2,1)S(1)}, bf16[8,128,128]{2,1,0:T(8,128)(2,1)S(1)}) custom-call(bf16[128,8,128]{2,1,0:T(8,128)(2,1)S(1)} %all_to_all.36.got, bf16[8,128,128]{2,1,0:T(8,128)(2,1)S(1)} %get-tuple-element.33.zn_in.zn, ...), custom_call_target="tpu_custom_call" | custom-call | flops 100663296 | bytes 2000000 | tf_op jit(solution)/shard_map/pallas_call | solution.py:302
  68.0 19.3 %all_to_all.37 = bf16[128,8,128]{2,1,0:T(8,128)(2,1)S(1)} all-to-all(bf16[128,8,128]{2,1,0:T(8,128)(2,1)S(1)} %get-tuple-element.35), channel_id=1, replica_groups={{0,1,2,3,4,5,6,7,8,9,10,11,12,13,14,15,32,33,34,35,36,37,38,39,40,41,42..., dimensions={0} | all-to-all | bytes 524288 | tf_op jit(solution)/shard_map/all_to_all | solution.py:257
  87.3 3.3 %collective-permute-start.1 = (bf16[128,8,128]{2,1,0:T(8,128)(2,1)S(1)}, bf16[128,8,128]{2,1,0:T(8,128)(2,1)S(1)}, u32[]{:S(2)}, u32[]{:S(2)}) collective-permute-start(bf16[128,8,128]{2,1,0:T(8,128)(2,1)S(1)} %all_to_all.37), channel_id=1, source_target_pairs={{0,16},{16,0},{32,48},{48,32},{64,80},{80,64},{96,112},{112,96},{1... | collective-permute-start | bytes 786440 | tf_op jit(solution)/shard_map/ppermute | solution.py:261
  90.6 1.2 collective-permute-done.1
  91.8 2.2 %shard_map.148 = bf16[8,4,4,2,8,128]{5,4,3,2,1,0:T(8,128)(2,1)} custom-call(bf16[8,4,4,8,128]{4,3,2,1,0:T(8,128)(2,1)S(1)} %bitcast.15, bf16[8,4,4,8,128]{4,3,2,1,0:T(8,128)(2,1)S(1)} %bitcast.17, bf16[256,512]{1,0:T(8,128)(2,1)S(1)} %get-tuple-element.36.left, bf16[256,512]{1,0:T(8,128)(2,1)S(1)} %get-tuple-element.37.right), custom_call_target="tpu_custom_call" | custom-call | flops 268435456 | bytes 2000000 | tf_op jit(solution)/shard_map/pallas_call | solution.py:326
  94.0 6.4 %all-to-all-start.3 = ((bf16[128,2,8,128]{3,2,1,0:T(8,128)(2,1)}), bf16[128,2,8,128]{3,2,1,0:T(8,128)(2,1)S(1)}, u32[]{:S(2)}, u32[]{:S(2)}) async-start(bf16[128,2,8,128]{3,2,1,0:T(8,128)(2,1)} %bitcast.9), calls=%async_computation.3 | async-start | bytes 1048576 | tf_op jit(solution)/shard_map/all_to_all | solution.py:257
  100.3 0.6 shard_map.149
  100.9 18.6 %all-to-all-done.3.got = bf16[128,2,8,128]{3,2,1,0:T(8,128)(2,1)S(1)} async-done(((bf16[128,2,8,128]{3,2,1,0:T(8,128)(2,1)}), bf16[128,2,8,128]{3,2,1,0:T(8,128)(2,1)S(1)}, u32[]{:S(2)}, u32[]{:S(2)}) %all-to-all-start.3) | async-done | bytes 524320 | tf_op jit(solution)/shard_map/all_to_all | solution.py:257
  119.5 1.2 shard_map.150
  120.6 13.8 %all_to_all.38.parts = bf16[32,32,128]{2,1,0:T(8,128)(2,1)S(1)} all-to-all(bf16[32,32,128]{2,1,0:T(8,128)(2,1)S(1)} %get-tuple-element.47), channel_id=1, replica_groups={{0,1,2,3,16,17,18,19,64,65,66,67,80,81,82,83,128,129,130,131,144,145,14..., dimensions={0} | all-to-all | bytes 524288 | tf_op jit(solution)/shard_map/all_to_all | solution.py:257
  134.5 9.5 %all_to_all.39.parts = bf16[8,32,128]{2,1,0:T(8,128)(2,1)S(1)} all-to-all(bf16[8,32,128]{2,1,0:T(8,128)(2,1)S(1)} %shard_map.152), channel_id=1, replica_groups={{0,32,4,36,8,40,12,44},{1,33,5,37,9,41,13,45},{2,34,6,38,10,42,14,46},{..., dimensions={0} | all-to-all | bytes 131072 | tf_op jit(solution)/shard_map/all_to_all | solution.py:257
  144.0 0.7 shard_map.153
  144.7 5.7 %all-to-all-start.6 = ((bf16[32,32,128]{2,1,0:T(8,128)(2,1)}), bf16[32,32,128]{2,1,0:T(8,128)(2,1)S(1)}, u32[]{:S(2)}, u32[]{:S(2)}) async-start(bf16[32,32,128]{2,1,0:T(8,128)(2,1)} %shard_map.153), calls=%async_computation.6 | async-start | bytes 524288 | tf_op jit(solution)/shard_map/all_to_all | solution.py:257
  150.4 2.5 %shard_map.151 = f32[4,8,32,128]{3,2,1,0:T(8,128)} custom-call(bf16[8,512,128]{2,1,0:T(8,128)(2,1)S(1)} %get-tuple-element.45.dproj, bf16[4,8,32,128]{3,2,1,0:T(8,128)(2,1)S(1)} %bitcast.19, f32[1,128]{1,0:T(1,128)S(1)} %bitcast.23, bf16[512,128]{1,0:T(8,128)(2,1)S(1)} %get-tuple-element.39.w_t, f32[8,128,128]{2,1,0:T(8,128)S(1)} %get-tuple-element.46.dzn_in), custom_call_target="tpu_custom_call" | custom-call | flops 134217728 | bytes 2000000 | tf_op jit(solution)/shard_map/pallas_call | solution.py:342
  152.9 6.4 %all-to-all-done.6.got = bf16[32,32,128]{2,1,0:T(8,128)(2,1)S(1)} async-done(((bf16[32,32,128]{2,1,0:T(8,128)(2,1)}), bf16[32,32,128]{2,1,0:T(8,128)(2,1)S(1)}, u32[]{:S(2)}, u32[]{:S(2)}) %all-to-all-start.6) | async-done | bytes 262176 | tf_op jit(solution)/shard_map/all_to_all | solution.py:257
  159.3 0.8 shard_map.154
  (12 shorter events, 0.1 us)
Async XLA Ops:
  0.6 0.7 copy-start.8
  0.6 0.7 copy-start.5
  1.3 1.0 copy-start.1
  2.3 0.9 copy-start.7
  3.2 0.7 copy-start.9
  41.6 4.6 %collective-permute-start = (f32[8,32,512]{2,1,0:T(8,128)S(1)}, f32[8,32,512]{2,1,0:T(8,128)S(1)}, u32[]{:S(2)}, u32[]{:S(2)}) collective-permute-start(f32[8,32,512]{2,1,0:T(8,128)S(1)} %get-tuple-element.32), channel_id=1, source_target_pairs={{0,16},{16,0},{32,48},{48,32},{64,80},{80,64},{96,112},{112,96},{1... | collective-permute-start | bytes 1572872 | tf_op jit(solution)/shard_map/ppermute | solution.py:261
  46.6 19.1 %copy-start = (bf16[32,32,128]{2,1,0:T(8,128)(2,1)S(1)}, bf16[32,32,128]{2,1,0:T(8,128)(2,1)}, u32[]{:S(2)}) copy-start(bf16[32,32,128]{2,1,0:T(8,128)(2,1)} %param.10) | copy-start | bytes 786436
  46.6 19.1 %copy-start.3 = (bf16[128,128]{1,0:T(8,128)(2,1)S(1)}, bf16[128,128]{1,0:T(8,128)(2,1)}, u32[]{:S(2)}) copy-start(bf16[128,128]{1,0:T(8,128)(2,1)} %w_gate.1) | copy-start | bytes 98308
  46.6 19.1 %copy-start.4 = (bf16[128,128]{1,0:T(8,128)(2,1)S(1)}, bf16[128,128]{1,0:T(8,128)(2,1)}, u32[]{:S(2)}) copy-start(bf16[128,128]{1,0:T(8,128)(2,1)} %w_out.1) | copy-start | bytes 98308
  65.7 0.7 copy-start.6
  87.3 4.5 %collective-permute-start.1 = (bf16[128,8,128]{2,1,0:T(8,128)(2,1)S(1)}, bf16[128,8,128]{2,1,0:T(8,128)(2,1)S(1)}, u32[]{:S(2)}, u32[]{:S(2)}) collective-permute-start(bf16[128,8,128]{2,1,0:T(8,128)(2,1)S(1)} %all_to_all.37), channel_id=1, source_target_pairs={{0,16},{16,0},{32,48},{48,32},{64,80},{80,64},{96,112},{112,96},{1... | collective-permute-start | bytes 786440 | tf_op jit(solution)/shard_map/ppermute | solution.py:261
  94.0 25.5 %all-to-all-start.3 = ((bf16[128,2,8,128]{3,2,1,0:T(8,128)(2,1)}), bf16[128,2,8,128]{3,2,1,0:T(8,128)(2,1)S(1)}, u32[]{:S(2)}, u32[]{:S(2)}) async-start(bf16[128,2,8,128]{3,2,1,0:T(8,128)(2,1)} %bitcast.9), calls=%async_computation.3 | async-start | bytes 1048576 | tf_op jit(solution)/shard_map/all_to_all | solution.py:257
  144.7 5.7 %copy-start.2 = (bf16[32,32,128]{2,1,0:T(8,128)(2,1)S(1)}, bf16[32,32,128]{2,1,0:T(8,128)(2,1)}, u32[]{:S(2)}) copy-start(bf16[32,32,128]{2,1,0:T(8,128)(2,1)} %param.9) | copy-start | bytes 786436
  144.7 14.6 %all-to-all-start.6 = ((bf16[32,32,128]{2,1,0:T(8,128)(2,1)}), bf16[32,32,128]{2,1,0:T(8,128)(2,1)S(1)}, u32[]{:S(2)}, u32[]{:S(2)}) async-start(bf16[32,32,128]{2,1,0:T(8,128)(2,1)} %shard_map.153), calls=%async_computation.6 | async-start | bytes 524288 | tf_op jit(solution)/shard_map/all_to_all | solution.py:257

commit v3 on v2

v3 whole, which is shorter than its diff:
```python
import jax
import jax.numpy as jnp
from jax import lax
from jax.experimental import pallas as pl
from jax.experimental.pallas import tpu as pltpu
from jax.sharding import PartitionSpec as P


BLOCK = 128
EPS = 1e-05
F32 = jnp.float32
BF16 = jnp.bfloat16
AXES = ("row", "col")
VMEM_LIMIT = 12 * 1024 * 1024


def dot(x, y, dims):
    return lax.dot_general(x, y, (dims, ((), ())), preferred_element_type=F32)


NN = ((1,), (0,))
NT = ((1,), (1,))
TN = ((0,), (0,))


def norm_rows(values, axis):
    centred = values - jnp.mean(values, axis=axis, keepdims=True)
    rstd = lax.rsqrt(jnp.mean(centred * centred, axis=axis, keepdims=True) + EPS)
    return centred * rstd, rstd


def norm_back(e, nhat, rstd, axis):
    first = jnp.mean(e, axis=axis, keepdims=True)
    second = jnp.mean(e * nhat, axis=axis, keepdims=True)
    return rstd * (e - first - nhat * second)


def swap_segments(v):
    lane = lax.broadcasted_iota(jnp.int32, v[0].shape, 1)
    low = lane < 64
    even = (lane // 32) % 2 == 0
    w = [None] * 4
    for m in range(2):
        w[m] = jnp.where(low, v[m], pltpu.roll(v[m + 2], 64, 1))
        w[m + 2] = jnp.where(low, pltpu.roll(v[m], 64, 1), v[m + 2])
    u = [None] * 4
    for m in (0, 2):
        u[m] = jnp.where(even, w[m], pltpu.roll(w[m + 1], 32, 1))
        u[m + 1] = jnp.where(even, pltpu.roll(w[m], 96, 1), w[m + 1])
    return u


def group(ref, t):
    return ref[:, t].reshape(128, 128)


def fetch(pairs, sems):
    copies = [pltpu.make_async_copy(far, near, sems.at[n]) for n, (far, near) in enumerate(pairs)]
    for copy in copies:
        copy.start()
    return copies


def project_kernel(
    pair_far, gain_far, chain_far, contact_far, w_far, chunks, zn_out, mask_out, w_t,
    left, right, pair, gain, chain, contact, w_in, sems
):
    copies = fetch(
        [(w_far, w_in), (gain_far, gain), (chain_far, chain), (contact_far, contact), (pair_far, pair)], sems
    )
    for copy in copies[:4]:
        copy.wait()
    w_t[...] = w_in[...].astype(F32).T.astype(BF16)
    row_start = lax.axis_index("row") * 32
    col_start = lax.axis_index("col") * 32
    lane = lax.broadcasted_iota(jnp.int32, (8, 128), 1)

    def chain_from(start):
        row = jnp.broadcast_to(chain[pl.ds(start // 128, 1), :], (8, 128)).astype(F32)
        return pltpu.roll(row, (128 - start % 128) % 128, 1)

    first = jnp.where(lane < 32, chain_from(col_start), 0.0)
    col_id = first + pltpu.roll(first, 32, 1) + pltpu.roll(first, 64, 1) + pltpu.roll(first, 96, 1)
    down = jnp.broadcast_to(chain_from(row_start)[:1], (128, 128)).T
    row_id = down[:8]
    for seg in range(1, 4):
        row_id = jnp.where(lane // 32 == seg, down[8 * seg : 8 * seg + 8], row_id)
    block = lax.broadcasted_iota(jnp.int32, (4, 4), 1) == row_start // BLOCK
    block = block & (lax.broadcasted_iota(jnp.int32, (4, 4), 0) == col_start // BLOCK)
    listed = jnp.sum(jnp.where(block, contact[...].astype(F32), 0.0), keepdims=True)
    mask = jnp.maximum(listed, jnp.where(row_id == col_id, 1.0, 0.0))
    mask_out[...] = mask
    copies[4].wait()
    for t in range(8):
        nhat, _ = norm_rows(group(pair, t).astype(F32), 1)
        zn = (nhat * gain[...]).astype(BF16)
        zn_out[t] = zn
        proj = dot(w_t[...], zn, NT)
        weight = mask[t : t + 1, :]
        left[:, t, :] = jax.nn.sigmoid(proj[128:256]) * proj[:128] * weight
        right[:, t, :] = jax.nn.sigmoid(proj[384:]) * proj[256:384] * weight
    chunks[:, 0] = left[...].astype(BF16)
    chunks[:, 1] = right[...].astype(BF16)


def column_of(row):
    return jnp.broadcast_to(row, (128, 128)).T


def gate_kernel(zn_in, cot, w_gate, w_out, out_gain, e_out):
    gain_col = column_of(out_gain[...])
    for t in range(8):
        gate = jax.nn.sigmoid(dot(zn_in[t], w_gate[...], NN))
        dout = (group(cot, t).astype(F32) * gate).astype(BF16)
        e_out[t] = dot(w_out[...], dout, NT) * gain_col


def slope_kernel(zn_in, w_t, mask, slopes):
    for t in range(8):
        proj = dot(w_t[...], zn_in[t], NT)
        weight = mask[t : t + 1, :]
        for n in (0, 256):
            gated = jax.nn.sigmoid(proj[n + 128 : n + 256])
            slopes[t, n : n + 128] = gated * weight
            slopes[t, n + 128 : n + 256] = gated * weight * proj[n : n + 128] * (1.0 - gated)


def product_kernel(got, keep, send, left, right, x_all):
    for hi in range(4):
        for ab, rows in enumerate((left, right)):
            u = swap_segments([got[:, hi, lo, ab].astype(F32).reshape(64, 128) for lo in range(4)])
            for m in range(4):
                rows[pl.ds(64 * m, 64), pl.ds(128 * hi, 128)] = u[m].astype(BF16)
    x_all[...] = dot(left[...], right[...], TN).reshape(8, 2, 32, 512)
    core = lax.axis_index("row") % 2
    keep[...] = x_all[:, core]
    send[...] = x_all[:, 1 - core]


def product_sum_kernel(keep, came, x_out):
    for hi in range(4):
        lanes = pl.ds(128 * hi, 128)
        u = swap_segments(
            [(keep[:, 8 * m : 8 * m + 8, lanes] + came[:, 8 * m : 8 * m + 8, lanes]).reshape(64, 128) for m in range(4)]
        )
        for lo in range(4):
            x_out[:, hi, lo] = u[lo].reshape(8, 8, 128).astype(BF16)


def output_kernel(got, e_in, out_gain, dx_out, xn_out, x_all, dx_all):
    gain_col = column_of(out_gain[...])
    x_all[...] = got[...].astype(F32)
    for t in range(8):
        xhat, xrstd = norm_rows(x_all[:, t, :], 0)
        dx_all[:, t, :] = norm_back(e_in[t], xhat, xrstd, 0)
        xn_out[t] = (xhat * gain_col).astype(BF16)
    dx_out[...] = dx_all[...].astype(BF16)


def output_grads_kernel(xn_in, cot, zn, w_gate, w_out, gain, out_gain, update, dzn, grads, gains):
    out_sum = jnp.zeros((128, 128), F32)
    gate_sum = jnp.zeros((128, 128), F32)
    for t in range(8):
        xn = xn_in[t]
        outp = dot(xn, w_out[...], TN)
        gate = jax.nn.sigmoid(dot(zn[t], w_gate[...], NN))
        dy = group(cot, t).astype(F32)
        dout = (dy * gate).astype(BF16)
        update[:, t] = (gate * outp).astype(BF16).reshape(4, 32, 128)
        dgpre = (dy * outp * gate * (1.0 - gate)).astype(BF16)
        out_sum += dot(xn, dout, NN)
        gate_sum += dot(dgpre, zn[t], TN)
        dzn[t] = dot(dgpre, w_gate[...], NT)
    grads[:128] = out_sum
    grads[128:] = gate_sum
    column = jnp.sum(out_sum * w_out[...].astype(F32), axis=1, keepdims=True) / column_of(out_gain[...])
    row = jnp.sum(gate_sum * w_gate[...].astype(F32).T, axis=0, keepdims=True) / gain[...]
    first = lax.broadcasted_iota(jnp.int32, (8, 128), 0) == 0
    gains[...] = jnp.where(first, row, column.T[:8])


def back_product_kernel(got, came, left, right, out, dx_rows, d_rows):
    core = lax.axis_index("row") % 2
    for hi in range(4):
        for source, place in ((got, core), (came, 1 - core)):
            u = swap_segments([source[:, hi, lo].astype(F32).reshape(64, 128) for lo in range(4)])
            for m in range(4):
                dx_rows[:, place, m, :, pl.ds(128 * hi, 128)] = u[m].reshape(8, 8, 128)
    dx = dx_rows[...].reshape(512, 512).astype(BF16)
    d_rows[0] = dot(right[...], dx, NT)
    d_rows[1] = dot(left[...], dx, NN)
    for hi in range(4):
        for ab in range(2):
            u = swap_segments([d_rows[ab, pl.ds(64 * m, 64), pl.ds(128 * hi, 128)] for m in range(4)])
            for lo in range(4):
                out[:, hi, lo, ab] = u[lo].reshape(8, 8, 128).astype(BF16)


def input_grads_kernel(
    got, zn, slopes, gain_far, w_t, early_far, early_gains_far, dproj_out, grads, d_left, d_right, gain, early, early_gains, sems
):
    copies = fetch([(gain_far, gain), (early_far, early), (early_gains_far, early_gains)], sems)
    total = jnp.zeros((512, 128), F32)
    d_left[...] = got[:, 0].astype(F32)
    d_right[...] = got[:, 1].astype(F32)
    for t in range(8):
        da, db = d_left[:, t, :], d_right[:, t, :]
        dproj = (jnp.concatenate([da, da, db, db], axis=0) * slopes[t]).astype(BF16)
        dproj_out[t] = dproj
        total += dot(dproj, zn[t], NN)
    for copy in copies:
        copy.wait()
    row = jnp.sum(total * w_t[...].astype(F32), axis=0, keepdims=True) / gain[...]
    first = lax.broadcasted_iota(jnp.int32, (8, 128), 0) == 0
    gains = early_gains[...] + jnp.where(first, row, 0.0)
    grads[...] = jnp.concatenate(
        [
            total.reshape(32, 16, 128),
            early[...].reshape(32, 8, 128),
            jnp.broadcast_to(gains[None], (32, 8, 128)),
        ],
        axis=1,
    ).astype(BF16)


def input_kernel(dproj, pair, gain, w_t, dzn_in, grad_pair):
    for t in range(8):
        nhat, rstd = norm_rows(group(pair, t).astype(F32), 1)
        dzn = dot(dproj[t], w_t[...], TN) + dzn_in[t]
        grad_pair[:, t] = norm_back(dzn * gain[...], nhat, rstd, 1).reshape(4, 32, 128)


def sum_kernel(parts, out):
    total = jnp.sum(parts[...].astype(F32), axis=0, keepdims=True)
    out[...] = jnp.broadcast_to(total, out.shape).astype(BF16)


def unpack_kernel(got, grad_in, grad_gate, grad_out, grad_gain, grad_out_gain):
    total = got[...].astype(F32)
    grad_in[...] = total[:, :16].reshape(512, 128).T
    early = total[:, 16:24].reshape(256, 128)
    grad_out[...] = early[:128]
    grad_gate[...] = early[128:].T
    grad_gain[...] = total[0, 24:25]
    grad_out_gain[...] = total[0, 25:26]


VMEM = pl.BlockSpec(memory_space=pltpu.VMEM)
FAR = pl.BlockSpec(memory_space=pltpu.HBM)


def far(array):
    return pltpu.with_memory_space_constraint(array, pltpu.HBM)


def call(kernel, inputs, outs, scratch, flops, far_inputs=(), far_outputs=()):
    fetched = [(inputs[n].shape, inputs[n].dtype) for n in far_inputs]
    semaphores = [pltpu.SemaphoreType.DMA((len(fetched),))] if fetched else []
    return pl.pallas_call(
        kernel,
        out_shape=[
            pltpu.HBM(shape, dtype) if n in far_outputs else jax.ShapeDtypeStruct(shape, dtype)
            for n, (shape, dtype) in enumerate(outs)
        ],
        in_specs=[FAR if n in far_inputs else VMEM for n in range(len(inputs))],
        out_specs=[VMEM] * len(outs),
        scratch_shapes=[pltpu.VMEM(shape, F32) for shape in scratch]
        + [pltpu.VMEM(shape, dtype) for shape, dtype in fetched]
        + semaphores,
        compiler_params=pltpu.CompilerParams(vmem_limit_bytes=VMEM_LIMIT),
        cost_estimate=pl.CostEstimate(flops=flops, bytes_accessed=2000000, transcendentals=0),
    )(*[far(array) if n in far_inputs else array for n, array in enumerate(inputs)])


def groups_by(place):
    found = {}
    for device in range(256):
        group_id, order = place(device // 16, device % 16)
        found.setdefault(group_id, []).append((order, device))
    return [[device for _, device in sorted(members)] for _, members in sorted(found.items())]


SAME_CORE = groups_by(lambda row, col: (row % 2, (row // 2, col)))
PLANE = groups_by(lambda row, col: ((col // 4, row // 2 % 2), (row // 4, row % 2, col % 4)))
LINE = groups_by(lambda row, col: ((row // 4, row % 2, col % 4), (col // 4, row // 2 % 2)))


def exchange(chunks, groups):
    return lax.all_to_all(chunks, AXES, 0, 0, tiled=True, axis_index_groups=groups)


def swap_cores(array):
    return lax.ppermute(array, "row", [(row, row ^ 1) for row in range(16)])


def sum_parts(parts, copies):
    return call(sum_kernel, [parts], [((copies, 32, 128), BF16)], [], 1000000)[0]


def on_device(pair, cotangent, contact, chain, gain_in, output_norm_gain, w_in, w_gate, w_out):
    pair4 = pair.reshape(4, 8, 32, 128)
    cot4 = cotangent.reshape(4, 8, 32, 128)
    gain = gain_in.reshape(1, 128)
    out_gain = output_norm_gain.reshape(1, 128)
    flat, flat_wide = ((8, 128, 128), BF16), ((8, 128, 128), F32)
    tiles, blocks = (128, 8, 128), (8, 4, 4, 8, 128)
    rows = ((256, 512), BF16)

    chunks, zn, mask, w_t = call(
        project_kernel,
        [pair4, gain, chain.reshape(4, 128), contact, w_in],
        [((128, 2, 8, 128), BF16), flat, ((8, 128), F32), ((512, 128), BF16)],
        [tiles, tiles],
        134217728,
        far_inputs=(0, 1, 2, 3, 4),
    )
    got = exchange(chunks, SAME_CORE).reshape(8, 4, 4, 2, 8, 128)
    keep, send, left, right = call(
        product_kernel,
        [got],
        [((8, 32, 512), F32), ((8, 32, 512), F32), rows, rows],
        [(8, 2, 32, 512)],
        134217728,
    )
    send, zn_then = lax.optimization_barrier((send, zn))
    (e,) = call(gate_kernel, [zn_then, cot4, w_gate, w_out, out_gain], [flat_wide], [], 67108864)
    came, e = lax.optimization_barrier((swap_cores(send), e))
    (x_chunks,) = call(product_sum_kernel, [keep, came], [(blocks, BF16)], [], 1000000)
    got = exchange(x_chunks.reshape(128, 8, 128), SAME_CORE)
    dx_chunks, xn = call(
        output_kernel, [got, e, out_gain], [((128, 8, 128), BF16), flat], [tiles, tiles], 1000000
    )
    got = exchange(dx_chunks, SAME_CORE)
    got, mask, xn = lax.optimization_barrier((got, mask, xn))
    came = swap_cores(got)
    (slopes,) = call(slope_kernel, [zn, w_t, mask], [((8, 512, 128), F32)], [], 134217728)
    update, dzn, early, early_gains = call(
        output_grads_kernel,
        [xn, cot4, zn, w_gate, w_out, gain, out_gain],
        [((4, 8, 32, 128), BF16), flat_wide, ((256, 128), F32), ((8, 128), F32)],
        [],
        134217728,
        far_outputs=(0, 1, 2, 3),
    )
    (d_chunks,) = call(
        back_product_kernel,
        [got.reshape(blocks), came.reshape(blocks), left, right],
        [((8, 4, 4, 2, 8, 128), BF16)],
        [(8, 2, 4, 8, 512), (2, 256, 512)],
        268435456,
    )
    got = exchange(d_chunks.reshape(128, 2, 8, 128), SAME_CORE)
    dproj, parts = call(
        input_grads_kernel,
        [got, zn, slopes, gain, w_t, early, early_gains],
        [((8, 512, 128), BF16), ((32, 32, 128), BF16)],
        [tiles, tiles],
        134217728,
        far_inputs=(3, 5, 6),
        far_outputs=(0, 1),
    )
    parts = exchange(parts, PLANE)
    (grad_pair,) = call(
        input_kernel, [dproj, pair4, gain, w_t, dzn], [((4, 8, 32, 128), F32)], [], 134217728
    )
    parts, grad_pair = lax.optimization_barrier((parts, grad_pair))
    parts = exchange(sum_parts(parts, 8), LINE)
    parts = exchange(sum_parts(parts, 32), PLANE)
    grad_w_in, grad_w_gate, grad_w_out, grad_gain, grad_out_gain = call(
        unpack_kernel,
        [parts],
        [((128, 512), F32), ((128, 128), F32), ((128, 128), F32), ((1, 128), F32), ((1, 128), F32)],
        [],
        1000000,
    )
    return (
        update.reshape(32, 32, 128),
        grad_pair.reshape(32, 32, 128),
        grad_w_in,
        grad_w_gate,
        grad_w_out,
        grad_gain.reshape(128),
        grad_out_gain.reshape(128),
    )


def solution(mesh):
    return jax.shard_map(
        on_device,
        mesh=mesh,
        in_specs=(P("row", "col", None), P("row", "col", None), P(), P(), P(), P(), P(), P(), P()),
        out_specs=(P("row", "col", None), P("row", "col", None), P(), P(), P(), P(), P()),
        check_vma=False,
    )
```

time: 161 us -> 157 us (0.975)
  waiting for transfers between devices: 27.7 us -> 21.4 us
  Pallas kernels: 13.4 us -> 17.2 us
    all_to_all x2, waiting for transfers between devices: 25 us -> 20.3 us  [exchange(): lax.all_to_all(chunks, AXES, 0, 0, tiled=True, axis_index_groups=groups)]
    pallas_call x11 -> x13, Pallas kernels: 13.4 us -> 17.2 us  [call(): pl.pallas_call(kernel, out_shape=[pltpu.HBM(shape, dtype) if n in far_out...]
  transfers between devices with their start and end apart: 4 -> 4, of which waited for: 4 -> 3; matrix products, arithmetic and copies ran while one was open for 0% -> 0% of each run, Pallas kernels for 2% -> 4%
where the time goes in v3:
time: 157 us
  blocking collectives  96.1 us (61%)
  waiting for transfers between devices  21.4 us (14%)
  starting transfers between devices  18.4 us (12%)
  Pallas kernels  17.2 us (11%)
  local copies, waits for them, and re-layouts  2.85 us (2%)
    all_to_all x5, blocking collectives, exchange(): lax.all_to_all(chunks, AXES, 0, 0, tiled=True, axis_index_groups=groups)  96.1 us
    all_to_all x2, waiting for transfers between devices, exchange(): lax.all_to_all(chunks, AXES, 0, 0, tiled=True, axis_index_groups=groups)  20.3 us
    pallas_call x13, Pallas kernels, call(): pl.pallas_call(kernel, out_shape=[pltpu.HBM(shape, dtype) if n in far_out...  17.2 us
    all_to_all x2, starting transfers between devices, exchange(): lax.all_to_all(chunks, AXES, 0, 0, tiled=True, axis_index_groups=groups)  12.1 us
    ppermute x2, starting transfers between devices, swap_cores(): return lax.ppermute(array, 'row', [(row, row ^ 1) for row in range(16)])  6.37 us
  transfers between devices with their start and end apart: 4, of which 3 were waited for; matrix products, arithmetic and copies ran while one was open for 0% of the time, Pallas kernels for 4%

profile of v3, /device:TPU:1, one launch (start us, length us, event | category | flops | bytes accessed | tf_op | source)
XLA Modules:
  0.0 156.9 jit_solution(736869633554823055)
XLA Ops:
  0.7 2.6 %shard_map.144 = (bf16[128,2,8,128]{3,2,1,0:T(8,128)(2,1)S(1)}, bf16[8,128,128]{2,1,0:T(8,128)(2,1)S(1)}, f32[8,128]{1,0:T(8,128)S(1)}, bf16[512,128]{1,0:T(8,128)(2,1)S(1)}) custom-call(bf16[4,8,32,128]{3,2,1,0:T(8,128)(2,1)} %bitcast.20, f32[1,128]{1,0:T(1,128)} %bitcast.25, s32[4,128]{1,0:T(4,128)} %bitcast.31, s32[4,4]{1,0:T(4,128)} %contact_far.1, ...), custom_call_target="tpu_custom_call" | custom-call | flops 134217728 | bytes 2000000 | tf_op jit(solution)/shard_map/pallas_call | solution.py:259
  3.2 0.0 copy-start.7
  3.3 34.4 %all_to_all.35 = bf16[128,2,8,128]{3,2,1,0:T(8,128)(2,1)S(1)} all-to-all(bf16[128,2,8,128]{3,2,1,0:T(8,128)(2,1)S(1)} %get-tuple-element.37), channel_id=1, replica_groups={{0,1,2,3,4,5,6,7,8,9,10,11,12,13,14,15,32,33,34,35,36,37,38,39,40,41,42..., dimensions={0} | all-to-all | bytes 1048576 | tf_op jit(solution)/shard_map/all_to_all | solution.py:289
  37.7 1.0 shard_map.145
  38.6 3.1 %collective-permute-start = (f32[8,32,512]{2,1,0:T(8,128)S(1)}, f32[8,32,512]{2,1,0:T(8,128)S(1)}, u32[]{:S(2)}, u32[]{:S(2)}) collective-permute-start(f32[8,32,512]{2,1,0:T(8,128)S(1)} %get-tuple-element.41), channel_id=1, source_target_pairs={{0,16},{16,0},{32,48},{48,32},{64,80},{80,64},{96,112},{112,96},{1... | collective-permute-start | bytes 1572872 | tf_op jit(solution)/shard_map/ppermute | solution.py:293
  41.7 0.0 copy-done.4
  41.7 0.6 copy-done.6
  42.4 0.9 shard_map.146.e_in
  43.2 0.0 collective-permute-done.came
  43.2 0.4 shard_map.147
  43.6 18.9 %all_to_all.36.got = bf16[128,8,128]{2,1,0:T(8,128)(2,1)S(1)} all-to-all(bf16[128,8,128]{2,1,0:T(8,128)(2,1)S(1)} %bitcast.15), channel_id=1, replica_groups={{0,1,2,3,4,5,6,7,8,9,10,11,12,13,14,15,32,33,34,35,36,37,38,39,40,41,42..., dimensions={0} | all-to-all | bytes 524288 | tf_op jit(solution)/shard_map/all_to_all | solution.py:289
  62.6 0.9 shard_map.148
  63.5 19.2 %all_to_all.37 = bf16[128,8,128]{2,1,0:T(8,128)(2,1)S(1)} all-to-all(bf16[128,8,128]{2,1,0:T(8,128)(2,1)S(1)} %get-tuple-element.45), channel_id=1, replica_groups={{0,1,2,3,4,5,6,7,8,9,10,11,12,13,14,15,32,33,34,35,36,37,38,39,40,41,42..., dimensions={0} | all-to-all | bytes 524288 | tf_op jit(solution)/shard_map/all_to_all | solution.py:289
  82.8 3.3 %collective-permute-start.1 = (bf16[128,8,128]{2,1,0:T(8,128)(2,1)S(1)}, bf16[128,8,128]{2,1,0:T(8,128)(2,1)S(1)}, u32[]{:S(2)}, u32[]{:S(2)}) collective-permute-start(bf16[128,8,128]{2,1,0:T(8,128)(2,1)S(1)} %all_to_all.37), channel_id=1, source_target_pairs={{0,16},{16,0},{32,48},{48,32},{64,80},{80,64},{96,112},{112,96},{1... | collective-permute-start | bytes 786440 | tf_op jit(solution)/shard_map/ppermute | solution.py:293
  86.1 1.2 collective-permute-done.1
  87.2 2.2 %shard_map.150 = bf16[8,4,4,2,8,128]{5,4,3,2,1,0:T(8,128)(2,1)} custom-call(bf16[8,4,4,8,128]{4,3,2,1,0:T(8,128)(2,1)S(1)} %bitcast.16, bf16[8,4,4,8,128]{4,3,2,1,0:T(8,128)(2,1)S(1)} %bitcast.19, bf16[256,512]{1,0:T(8,128)(2,1)S(1)} %get-tuple-element.51.left, bf16[256,512]{1,0:T(8,128)(2,1)S(1)} %get-tuple-element.52.right), custom_call_target="tpu_custom_call" | custom-call | flops 268435456 | bytes 2000000 | tf_op jit(solution)/shard_map/pallas_call | solution.py:259
  89.4 6.3 %all-to-all-start.3 = ((bf16[128,2,8,128]{3,2,1,0:T(8,128)(2,1)}), bf16[128,2,8,128]{3,2,1,0:T(8,128)(2,1)S(1)}, u32[]{:S(2)}, u32[]{:S(2)}) async-start(bf16[128,2,8,128]{3,2,1,0:T(8,128)(2,1)} %bitcast.10), calls=%async_computation.3 | async-start | bytes 1048576 | tf_op jit(solution)/shard_map/all_to_all | solution.py:289
  95.8 2.6 %shard_map.149 = (bf16[4,8,32,128]{3,2,1,0:T(8,128)(2,1)}, f32[8,128,128]{2,1,0:T(8,128)}, f32[256,128]{1,0:T(8,128)}, f32[8,128]{1,0:T(8,128)}) custom-call(bf16[8,128,128]{2,1,0:T(8,128)(2,1)S(1)} %get-tuple-element.48.xn_in, bf16[4,8,32,128]{3,2,1,0:T(8,128)(2,1)S(1)} %bitcast.18, bf16[8,128,128]{2,1,0:T(8,128)(2,1)S(1)} %get-tuple-element.42.zn_in.zn, ...), custom_call_target="tpu_custom_call" | custom-call | flops 134217728 | bytes 2000000 | tf_op jit(solution)/shard_map/pallas_call | solution.py:259
  98.4 0.5 shard_map.151.slopes
  98.9 0.0 copy-start.2
  98.9 0.0 copy-start.9
  98.9 16.0 %all-to-all-done.3.got = bf16[128,2,8,128]{3,2,1,0:T(8,128)(2,1)S(1)} async-done(((bf16[128,2,8,128]{3,2,1,0:T(8,128)(2,1)}), bf16[128,2,8,128]{3,2,1,0:T(8,128)(2,1)S(1)}, u32[]{:S(2)}, u32[]{:S(2)}) %all-to-all-start.3) | async-done | bytes 524320 | tf_op jit(solution)/shard_map/all_to_all | solution.py:289
  114.9 2.7 %shard_map.152 = (bf16[8,512,128]{2,1,0:T(8,128)(2,1)}, bf16[32,32,128]{2,1,0:T(8,128)(2,1)}) custom-call(bf16[128,2,8,128]{3,2,1,0:T(8,128)(2,1)S(1)} %all-to-all-done.3.got, bf16[8,128,128]{2,1,0:T(8,128)(2,1)S(1)} %get-tuple-element.42.zn_in.zn, f32[8,512,128]{2,1,0:T(8,128)S(1)} %shard_map.151.slopes, f32[1,128]{1,0:T(1,128)} %bitcast.26, ...), custom_call_target="tpu_custom_call" | custom-call | flops 134217728 | bytes 2000000 | tf_op jit(solution)/shard_map/pallas_call | solution.py:259
  117.6 5.7 %all-to-all-start.4 = ((bf16[32,32,128]{2,1,0:T(8,128)(2,1)}), bf16[32,32,128]{2,1,0:T(8,128)(2,1)S(1)}, u32[]{:S(2)}, u32[]{:S(2)}) async-start(bf16[32,32,128]{2,1,0:T(8,128)(2,1)} %get-tuple-element.57), calls=%async_computation.4 | async-start | bytes 524288 | tf_op jit(solution)/shard_map/all_to_all | solution.py:289
  123.4 0.0 copy-done.2
  123.4 1.2 copy-done
  124.6 0.9 copy-done.3
  125.6 2.5 %shard_map.153 = f32[4,8,32,128]{3,2,1,0:T(8,128)} custom-call(bf16[8,512,128]{2,1,0:T(8,128)(2,1)S(1)} %copy-done, bf16[4,8,32,128]{3,2,1,0:T(8,128)(2,1)S(1)} %bitcast.21, f32[1,128]{1,0:T(1,128)S(1)} %bitcast.28, bf16[512,128]{1,0:T(8,128)(2,1)S(1)} %get-tuple-element.53.w_t, f32[8,128,128]{2,1,0:T(8,128)S(1)} %copy-done.2), custom_call_target="tpu_custom_call" | custom-call | flops 134217728 | bytes 2000000 | tf_op jit(solution)/shard_map/pallas_call | solution.py:259
  128.1 4.3 %all-to-all-done.4.parts = bf16[32,32,128]{2,1,0:T(8,128)(2,1)S(1)} async-done(((bf16[32,32,128]{2,1,0:T(8,128)(2,1)}), bf16[32,32,128]{2,1,0:T(8,128)(2,1)S(1)}, u32[]{:S(2)}, u32[]{:S(2)}) %all-to-all-start.4) | async-done | bytes 262176 | tf_op jit(solution)/shard_map/all_to_all | solution.py:289
  132.4 9.5 %all_to_all.38.parts = bf16[8,32,128]{2,1,0:T(8,128)(2,1)S(1)} all-to-all(bf16[8,32,128]{2,1,0:T(8,128)(2,1)S(1)} %shard_map.154), channel_id=1, replica_groups={{0,32,4,36,8,40,12,44},{1,33,5,37,9,41,13,45},{2,34,6,38,10,42,14,46},{..., dimensions={0} | all-to-all | bytes 131072 | tf_op jit(solution)/shard_map/all_to_all | solution.py:289
  142.0 14.0 %all_to_all.39.got = bf16[32,32,128]{2,1,0:T(8,128)(2,1)S(1)} all-to-all(bf16[32,32,128]{2,1,0:T(8,128)(2,1)S(1)} %shard_map.155), channel_id=1, replica_groups={{0,1,2,3,16,17,18,19,64,65,66,67,80,81,82,83,128,129,130,131,144,145,14..., dimensions={0} | all-to-all | bytes 524288 | tf_op jit(solution)/shard_map/all_to_all | solution.py:289
  156.0 0.8 shard_map.156
  (14 shorter events, 0.1 us)
Async XLA Ops:
  0.6 41.1 %copy-start.5 = (bf16[128,128]{1,0:T(8,128)(2,1)S(1)}, bf16[128,128]{1,0:T(8,128)(2,1)}, u32[]{:S(2)}) copy-start(bf16[128,128]{1,0:T(8,128)(2,1)} %w_out.3) | copy-start | bytes 98308
  0.6 41.0 %copy-start.4 = (bf16[128,128]{1,0:T(8,128)(2,1)S(1)}, bf16[128,128]{1,0:T(8,128)(2,1)}, u32[]{:S(2)}) copy-start(bf16[128,128]{1,0:T(8,128)(2,1)} %w_gate.3) | copy-start | bytes 98308
  0.7 41.0 %copy-start.1 = (bf16[32,32,128]{2,1,0:T(8,128)(2,1)S(1)}, bf16[32,32,128]{2,1,0:T(8,128)(2,1)}, u32[]{:S(2)}) copy-start(bf16[32,32,128]{2,1,0:T(8,128)(2,1)} %param.10) | copy-start | bytes 786436
  3.2 59.4 %copy-start.7 = (f32[128]{0:T(128)S(1)}, f32[128]{0:T(128)}, u32[]{:S(2)}) copy-start(f32[128]{0:T(128)} %param.14) | copy-start | bytes 1540
  38.6 4.6 %collective-permute-start = (f32[8,32,512]{2,1,0:T(8,128)S(1)}, f32[8,32,512]{2,1,0:T(8,128)S(1)}, u32[]{:S(2)}, u32[]{:S(2)}) collective-permute-start(f32[8,32,512]{2,1,0:T(8,128)S(1)} %get-tuple-element.41), channel_id=1, source_target_pairs={{0,16},{16,0},{32,48},{48,32},{64,80},{80,64},{96,112},{112,96},{1... | collective-permute-start | bytes 1572872 | tf_op jit(solution)/shard_map/ppermute | solution.py:293
  41.7 0.7 copy-start.6
  62.6 33.2 %copy-start.8 = (f32[128]{0:T(128)S(1)}, f32[128]{0:T(128)}, u32[]{:S(2)}) copy-start(f32[128]{0:T(128)} %param.13) | copy-start | bytes 1540
  82.8 4.5 %collective-permute-start.1 = (bf16[128,8,128]{2,1,0:T(8,128)(2,1)S(1)}, bf16[128,8,128]{2,1,0:T(8,128)(2,1)S(1)}, u32[]{:S(2)}, u32[]{:S(2)}) collective-permute-start(bf16[128,8,128]{2,1,0:T(8,128)(2,1)S(1)} %all_to_all.37), channel_id=1, source_target_pairs={{0,16},{16,0},{32,48},{48,32},{64,80},{80,64},{96,112},{112,96},{1... | collective-permute-start | bytes 786440 | tf_op jit(solution)/shard_map/ppermute | solution.py:293
  89.4 25.5 %all-to-all-start.3 = ((bf16[128,2,8,128]{3,2,1,0:T(8,128)(2,1)}), bf16[128,2,8,128]{3,2,1,0:T(8,128)(2,1)S(1)}, u32[]{:S(2)}, u32[]{:S(2)}) async-start(bf16[128,2,8,128]{3,2,1,0:T(8,128)(2,1)} %bitcast.10), calls=%async_computation.3 | async-start | bytes 1048576 | tf_op jit(solution)/shard_map/all_to_all | solution.py:289
  98.9 24.5 %copy-start.2 = (f32[8,128,128]{2,1,0:T(8,128)S(1)}, f32[8,128,128]{2,1,0:T(8,128)}, u32[]{:S(2)}) copy-start(f32[8,128,128]{2,1,0:T(8,128)} %get-tuple-element.59.dzn_in) | copy-start | bytes 1572868
  98.9 24.5 %copy-start.9 = (f32[128]{0:T(128)S(1)}, f32[128]{0:T(128)}, u32[]{:S(2)}) copy-start(f32[128]{0:T(128)} %param.13) | copy-start | bytes 1540
  117.6 14.7 %all-to-all-start.4 = ((bf16[32,32,128]{2,1,0:T(8,128)(2,1)}), bf16[32,32,128]{2,1,0:T(8,128)(2,1)S(1)}, u32[]{:S(2)}, u32[]{:S(2)}) async-start(bf16[32,32,128]{2,1,0:T(8,128)(2,1)} %get-tuple-element.57), calls=%async_computation.4 | async-start | bytes 524288 | tf_op jit(solution)/shard_map/all_to_all | solution.py:289
  123.4 1.2 copy-start
  124.6 0.9 copy-start.3

commit v4 on v3

--- a/solution.py
+++ b/solution.py
@@ -62,14 +62,24 @@
 
 
 def project_kernel(
-    pair_far, gain_far, chain_far, contact_far, w_far, chunks, zn_out, mask_out, w_t,
-    left, right, pair, gain, chain, contact, w_in, sems
+    pair_far, gain_far, chain_far, contact_far, w_far, out_gain_far, chunks, zn_out, mask_out, w_t, gains_out,
+    left, right, pair, gain, chain, contact, w_in, out_gain, sems
 ):
     copies = fetch(
-        [(w_far, w_in), (gain_far, gain), (chain_far, chain), (contact_far, contact), (pair_far, pair)], sems
-    )
-    for copy in copies[:4]:
+        [
+            (w_far, w_in),
+            (gain_far, gain),
+            (chain_far, chain),
+            (contact_far, contact),
+            (out_gain_far, out_gain),
+            (pair_far, pair),
+        ],
+        sems,
+    )
+    for copy in copies[:5]:
         copy.wait()
+    gains_out[0:8] = jnp.broadcast_to(gain[...], (8, 128))
+    gains_out[8:16] = jnp.broadcast_to(out_gain[...], (8, 128))
     w_t[...] = w_in[...].astype(F32).T.astype(BF16)
     row_start = lax.axis_index("row") * 32
     col_start = lax.axis_index("col") * 32
@@ -90,7 +100,7 @@
     listed = jnp.sum(jnp.where(block, contact[...].astype(F32), 0.0), keepdims=True)
     mask = jnp.maximum(listed, jnp.where(row_id == col_id, 1.0, 0.0))
     mask_out[...] = mask
-    copies[4].wait()
+    copies[5].wait()
     for t in range(8):
         nhat, _ = norm_rows(group(pair, t).astype(F32), 1)
         zn = (nhat * gain[...]).astype(BF16)
@@ -107,8 +117,8 @@
     return jnp.broadcast_to(row, (128, 128)).T
 
 
-def gate_kernel(zn_in, cot, w_gate, w_out, out_gain, e_out):
-    gain_col = column_of(out_gain[...])
+def gate_kernel(zn_in, cot, w_gate, w_out, both_gains, e_out):
+    gain_col = column_of(both_gains[8:9])
     for t in range(8):
         gate = jax.nn.sigmoid(dot(zn_in[t], w_gate[...], NN))
         dout = (group(cot, t).astype(F32) * gate).astype(BF16)
@@ -147,8 +157,8 @@
             x_out[:, hi, lo] = u[lo].reshape(8, 8, 128).astype(BF16)
 
 
-def output_kernel(got, e_in, out_gain, dx_out, xn_out, x_all, dx_all):
-    gain_col = column_of(out_gain[...])
+def output_kernel(got, e_in, both_gains, dx_out, xn_out, x_all, dx_all):
+    gain_col = column_of(both_gains[8:9])
     x_all[...] = got[...].astype(F32)
     for t in range(8):
         xhat, xrstd = norm_rows(x_all[:, t, :], 0)
@@ -157,7 +167,7 @@
     dx_out[...] = dx_all[...].astype(BF16)
 
 
-def output_grads_kernel(xn_in, cot, zn, w_gate, w_out, gain, out_gain, update, dzn, grads, gains):
+def output_grads_kernel(xn_in, cot, zn, w_gate, w_out, both_gains, update, dzn, grads, gains):
     out_sum = jnp.zeros((128, 128), F32)
     gate_sum = jnp.zeros((128, 128), F32)
     for t in range(8):
@@ -173,8 +183,8 @@
         dzn[t] = dot(dgpre, w_gate[...], NT)
     grads[:128] = out_sum
     grads[128:] = gate_sum
-    column = jnp.sum(out_sum * w_out[...].astype(F32), axis=1, keepdims=True) / column_of(out_gain[...])
-    row = jnp.sum(gate_sum * w_gate[...].astype(F32).T, axis=0, keepdims=True) / gain[...]
+    column = jnp.sum(out_sum * w_out[...].astype(F32), axis=1, keepdims=True) / column_of(both_gains[8:9])
+    row = jnp.sum(gate_sum * w_gate[...].astype(F32).T, axis=0, keepdims=True) / both_gains[0:1]
     first = lax.broadcasted_iota(jnp.int32, (8, 128), 0) == 0
     gains[...] = jnp.where(first, row, column.T[:8])
 
@@ -196,10 +206,7 @@
                 out[:, hi, lo, ab] = u[lo].reshape(8, 8, 128).astype(BF16)
 
 
-def input_grads_kernel(
-    got, zn, slopes, gain_far, w_t, early_far, early_gains_far, dproj_out, grads, d_left, d_right, gain, early, early_gains, sems
-):
-    copies = fetch([(gain_far, gain), (early_far, early), (early_gains_far, early_gains)], sems)
+def input_grads_kernel(got, zn, slopes, both_gains, w_t, early, early_gains, dproj_out, grads, d_left, d_right):
     total = jnp.zeros((512, 128), F32)
     d_left[...] = got[:, 0].astype(F32)
     d_right[...] = got[:, 1].astype(F32)
@@ -208,9 +215,7 @@
         dproj = (jnp.concatenate([da, da, db, db], axis=0) * slopes[t]).astype(BF16)
         dproj_out[t] = dproj
         total += dot(dproj, zn[t], NN)
-    for copy in copies:
-        copy.wait()
-    row = jnp.sum(total * w_t[...].astype(F32), axis=0, keepdims=True) / gain[...]
+    row = jnp.sum(total * w_t[...].astype(F32), axis=0, keepdims=True) / both_gains[0:1]
     first = lax.broadcasted_iota(jnp.int32, (8, 128), 0) == 0
     gains = early_gains[...] + jnp.where(first, row, 0.0)
     grads[...] = jnp.concatenate(
@@ -223,11 +228,11 @@
     ).astype(BF16)
 
 
-def input_kernel(dproj, pair, gain, w_t, dzn_in, grad_pair):
+def input_kernel(dproj, pair, both_gains, w_t, dzn_in, grad_pair):
     for t in range(8):
         nhat, rstd = norm_rows(group(pair, t).astype(F32), 1)
         dzn = dot(dproj[t], w_t[...], TN) + dzn_in[t]
-        grad_pair[:, t] = norm_back(dzn * gain[...], nhat, rstd, 1).reshape(4, 32, 128)
+        grad_pair[:, t] = norm_back(dzn * both_gains[0:1], nhat, rstd, 1).reshape(4, 32, 128)
 
 
 def sum_kernel(parts, out):
@@ -253,13 +258,21 @@
     return pltpu.with_memory_space_constraint(array, pltpu.HBM)
 
 
-def call(kernel, inputs, outs, scratch, flops, far_inputs=(), far_outputs=()):
+def near(array):
+    return pltpu.with_memory_space_constraint(array, pltpu.VMEM)
+
+
+def call(kernel, inputs, outs, scratch, flops, far_inputs=(), far_outputs=(), near_outputs=()):
     fetched = [(inputs[n].shape, inputs[n].dtype) for n in far_inputs]
     semaphores = [pltpu.SemaphoreType.DMA((len(fetched),))] if fetched else []
     return pl.pallas_call(
         kernel,
         out_shape=[
-            pltpu.HBM(shape, dtype) if n in far_outputs else jax.ShapeDtypeStruct(shape, dtype)
+            pltpu.HBM(shape, dtype)
+            if n in far_outputs
+            else pltpu.VMEM(shape, dtype)
+            if n in near_outputs
+            else jax.ShapeDtypeStruct(shape, dtype)
             for n, (shape, dtype) in enumerate(outs)
         ],
         in_specs=[FAR if n in far_inputs else VMEM for n in range(len(inputs))],
@@ -306,13 +319,14 @@
     tiles, blocks = (128, 8, 128), (8, 4, 4, 8, 128)
     rows = ((256, 512), BF16)
 
-    chunks, zn, mask, w_t = call(
+    chunks, zn, mask, w_t, gains = call(
         project_kernel,
-        [pair4, gain, chain.reshape(4, 128), contact, w_in],
-        [((128, 2, 8, 128), BF16), flat, ((8, 128), F32), ((512, 128), BF16)],
+        [pair4, gain, chain.reshape(4, 128), contact, w_in, out_gain],
+        [((128, 2, 8, 128), BF16), flat, ((8, 128), F32), ((512, 128), BF16), ((16, 128), F32)],
         [tiles, tiles],
         134217728,
-        far_inputs=(0, 1, 2, 3, 4),
+        far_inputs=(0, 1, 2, 3, 4, 5),
+        near_outputs=(4,),
     )
     got = exchange(chunks, SAME_CORE).reshape(8, 4, 4, 2, 8, 128)
     keep, send, left, right = call(
@@ -323,25 +337,27 @@
         134217728,
     )
     send, zn_then = lax.optimization_barrier((send, zn))
-    (e,) = call(gate_kernel, [zn_then, cot4, w_gate, w_out, out_gain], [flat_wide], [], 67108864)
-    came, e = lax.optimization_barrier((swap_cores(send), e))
+    (e,) = call(gate_kernel, [zn_then, cot4, w_gate, w_out, gains], [flat_wide], [], 67108864)
+    (slopes,) = call(slope_kernel, [zn_then, w_t, mask], [((8, 512, 128), F32)], [], 134217728)
+    came, e, slopes = lax.optimization_barrier((swap_cores(send), e, slopes))
     (x_chunks,) = call(product_sum_kernel, [keep, came], [(blocks, BF16)], [], 1000000)
     got = exchange(x_chunks.reshape(128, 8, 128), SAME_CORE)
     dx_chunks, xn = call(
-        output_kernel, [got, e, out_gain], [((128, 8, 128), BF16), flat], [tiles, tiles], 1000000
+        output_kernel, [got, e, gains], [((128, 8, 128), BF16), flat], [tiles, tiles], 1000000
     )
     got = exchange(dx_chunks, SAME_CORE)
-    got, mask, xn = lax.optimization_barrier((got, mask, xn))
+    got, xn = lax.optimization_barrier((got, xn))
     came = swap_cores(got)
-    (slopes,) = call(slope_kernel, [zn, w_t, mask], [((8, 512, 128), F32)], [], 134217728)
     update, dzn, early, early_gains = call(
         output_grads_kernel,
-        [xn, cot4, zn, w_gate, w_out, gain, out_gain],
+        [xn, cot4, zn, w_gate, w_out, gains],
         [((4, 8, 32, 128), BF16), flat_wide, ((256, 128), F32), ((8, 128), F32)],
         [],
         134217728,
-        far_outputs=(0, 1, 2, 3),
-    )
+        far_outputs=(0, 1),
+        near_outputs=(2, 3),
+    )
+    came, update, dzn, early, early_gains = lax.optimization_barrier((came, update, dzn, early, early_gains))
     (d_chunks,) = call(
         back_product_kernel,
         [got.reshape(blocks), came.reshape(blocks), left, right],
@@ -352,16 +368,15 @@
     got = exchange(d_chunks.reshape(128, 2, 8, 128), SAME_CORE)
     dproj, parts = call(
         input_grads_kernel,
-        [got, zn, slopes, gain, w_t, early, early_gains],
+        [got, zn, slopes, gains, w_t, near(early), near(early_gains)],
         [((8, 512, 128), BF16), ((32, 32, 128), BF16)],
         [tiles, tiles],
         134217728,
-        far_inputs=(3, 5, 6),
         far_outputs=(0, 1),
     )
     parts = exchange(parts, PLANE)
     (grad_pair,) = call(
-        input_kernel, [dproj, pair4, gain, w_t, dzn], [((4, 8, 32, 128), F32)], [], 134217728
+        input_kernel, [dproj, pair4, gains, w_t, dzn], [((4, 8, 32, 128), F32)], [], 134217728
     )
     parts, grad_pair = lax.optimization_barrier((parts, grad_pair))
     parts = exchange(sum_parts(parts, 8), LINE)

time: 157 us -> 156 us (level)
  blocking collectives: 96.1 us -> 121 us
  waiting for transfers between devices: 21.4 us -> 5.42 us
  starting transfers between devices: 18.4 us -> 11.7 us
  local copies, waits for them, and re-layouts: 2.85 us -> 1.24 us
  Pallas kernels: 17.2 us -> 15.6 us
    all_to_all x5 -> x6, blocking collectives: 96.1 us -> 121 us  [exchange(): lax.all_to_all(chunks, AXES, 0, 0, tiled=True, axis_index_groups=groups)]
    all_to_all x2 -> x1, waiting for transfers between devices: 20.3 us -> 5.24 us  [exchange(): lax.all_to_all(chunks, AXES, 0, 0, tiled=True, axis_index_groups=groups)]
    all_to_all x2 -> x1, starting transfers between devices: 12.1 us -> 5.31 us  [exchange(): lax.all_to_all(chunks, AXES, 0, 0, tiled=True, axis_index_groups=groups)]
    unnamed x20 -> x12, local copies, waits for them, and re-layouts: 2.85 us -> 1.24 us
  transfers between devices with their start and end apart: 4 -> 3, of which waited for: 3 -> 2; matrix products, arithmetic and copies ran while one was open for 0% -> 0% of each run, Pallas kernels for 4% -> 4%
where the time goes in v4:
time: 156 us
  blocking collectives  121 us (78%)
  Pallas kernels  15.6 us (10%)
  starting transfers between devices  11.7 us (8%)
  waiting for transfers between devices  5.42 us (3%)
    all_to_all x6, blocking collectives, exchange(): lax.all_to_all(chunks, AXES, 0, 0, tiled=True, axis_index_groups=groups)  121 us
    pallas_call x13, Pallas kernels, call(): pl.pallas_call(kernel, out_shape=[pltpu.HBM(shape, dtype) if n in far_out...  15.6 us
    ppermute x2, starting transfers between devices, swap_cores(): return lax.ppermute(array, 'row', [(row, row ^ 1) for row in range(16)])  6.36 us
    all_to_all x1, starting transfers between devices, exchange(): lax.all_to_all(chunks, AXES, 0, 0, tiled=True, axis_index_groups=groups)  5.31 us
    all_to_all x1, waiting for transfers between devices, exchange(): lax.all_to_all(chunks, AXES, 0, 0, tiled=True, axis_index_groups=groups)  5.24 us
  transfers between devices with their start and end apart: 3, of which 2 were waited for; matrix products, arithmetic and copies ran while one was open for 0% of the time, Pallas kernels for 4%

profile of v4, /device:TPU:1, one launch (start us, length us, event | category | flops | bytes accessed | tf_op | source)
XLA Modules:
  0.0 155.9 jit_solution(17639227587104547467)
XLA Ops:
  0.6 0.0 copy-start.5
  0.6 0.0 copy-start.4
  0.7 0.0 copy-start
  0.7 2.6 %shard_map.144 = (bf16[128,2,8,128]{3,2,1,0:T(8,128)(2,1)S(1)}, bf16[8,128,128]{2,1,0:T(8,128)(2,1)S(1)}, f32[8,128]{1,0:T(8,128)S(1)}, bf16[512,128]{1,0:T(8,128)(2,1)S(1)}, f32[16,128]{1,0:T(8,128)S(1)}) custom-call(bf16[4,8,32,128]{3,2,1,0:T(8,128)(2,1)} %bitcast.20, f32[1,128]{1,0:T(1,128)} %bitcast.26, s32[4,128]{1,0:T(4,128)} %bitcast.25, ...), custom_call_target="tpu_custom_call" | custom-call | flops 134217728 | bytes 2000000 | tf_op jit(solution)/shard_map/pallas_call | solution.py:268
  3.3 34.4 %all_to_all.35 = bf16[128,2,8,128]{3,2,1,0:T(8,128)(2,1)S(1)} all-to-all(bf16[128,2,8,128]{3,2,1,0:T(8,128)(2,1)S(1)} %get-tuple-element.43), channel_id=1, replica_groups={{0,1,2,3,4,5,6,7,8,9,10,11,12,13,14,15,32,33,34,35,36,37,38,39,40,41,42..., dimensions={0} | all-to-all | bytes 1048576 | tf_op jit(solution)/shard_map/all_to_all | solution.py:302
  37.7 1.0 shard_map.145
  38.6 3.1 %collective-permute-start = (f32[8,32,512]{2,1,0:T(8,128)S(1)}, f32[8,32,512]{2,1,0:T(8,128)S(1)}, u32[]{:S(2)}, u32[]{:S(2)}) collective-permute-start(f32[8,32,512]{2,1,0:T(8,128)S(1)} %get-tuple-element.47), channel_id=1, source_target_pairs={{0,16},{16,0},{32,48},{48,32},{64,80},{80,64},{96,112},{112,96},{1... | collective-permute-start | bytes 1572872 | tf_op jit(solution)/shard_map/ppermute | solution.py:306
  41.7 0.0 copy-done.5
  41.7 0.0 copy-done.4
  41.7 0.0 copy-done
  41.7 0.9 shard_map.146.e_in
  42.6 0.5 shard_map.147.slopes
  43.1 0.2 collective-permute-done.came
  43.2 0.4 shard_map.148
  43.6 18.9 %all_to_all.36.got = bf16[128,8,128]{2,1,0:T(8,128)(2,1)S(1)} all-to-all(bf16[128,8,128]{2,1,0:T(8,128)(2,1)S(1)} %bitcast.18), channel_id=1, replica_groups={{0,1,2,3,4,5,6,7,8,9,10,11,12,13,14,15,32,33,34,35,36,37,38,39,40,41,42..., dimensions={0} | all-to-all | bytes 524288 | tf_op jit(solution)/shard_map/all_to_all | solution.py:302
  62.5 0.9 shard_map.149
  63.5 19.3 %all_to_all.37 = bf16[128,8,128]{2,1,0:T(8,128)(2,1)S(1)} all-to-all(bf16[128,8,128]{2,1,0:T(8,128)(2,1)S(1)} %get-tuple-element.54), channel_id=1, replica_groups={{0,1,2,3,4,5,6,7,8,9,10,11,12,13,14,15,32,33,34,35,36,37,38,39,40,41,42..., dimensions={0} | all-to-all | bytes 524288 | tf_op jit(solution)/shard_map/all_to_all | solution.py:302
  82.8 3.3 %collective-permute-start.1 = (bf16[128,8,128]{2,1,0:T(8,128)(2,1)S(1)}, bf16[128,8,128]{2,1,0:T(8,128)(2,1)S(1)}, u32[]{:S(2)}, u32[]{:S(2)}) collective-permute-start(bf16[128,8,128]{2,1,0:T(8,128)(2,1)S(1)} %all_to_all.37), channel_id=1, source_target_pairs={{0,16},{16,0},{32,48},{48,32},{64,80},{80,64},{96,112},{112,96},{1... | collective-permute-start | bytes 786440 | tf_op jit(solution)/shard_map/ppermute | solution.py:306
  86.1 2.7 %shard_map.150 = (bf16[4,8,32,128]{3,2,1,0:T(8,128)(2,1)}, f32[8,128,128]{2,1,0:T(8,128)}, f32[256,128]{1,0:T(8,128)S(1)}, f32[8,128]{1,0:T(8,128)S(1)}) custom-call(bf16[8,128,128]{2,1,0:T(8,128)(2,1)S(1)} %get-tuple-element.57.xn_in, bf16[4,8,32,128]{3,2,1,0:T(8,128)(2,1)S(1)} %bitcast.17, bf16[8,128,128]{2,1,0:T(8,128)(2,1)S(1)} %get-tuple-element.48.zn_in.zn, ...), custom_call_target="tpu_custom_call" | custom-call | flops 134217728 | bytes 2000000 | tf_op jit(solution)/shard_map/pallas_call | solution.py:268
  88.8 0.0 collective-permute-done.1
  88.8 1.4 shard_map.151
  90.2 25.1 %all_to_all.38.got = bf16[128,2,8,128]{3,2,1,0:T(8,128)(2,1)S(1)} all-to-all(bf16[128,2,8,128]{3,2,1,0:T(8,128)(2,1)S(1)} %bitcast.14), channel_id=1, replica_groups={{0,1,2,3,4,5,6,7,8,9,10,11,12,13,14,15,32,33,34,35,36,37,38,39,40,41,42..., dimensions={0} | all-to-all | bytes 1048576 | tf_op jit(solution)/shard_map/all_to_all | solution.py:302
  115.3 1.9 %shard_map.152 = (bf16[8,512,128]{2,1,0:T(8,128)(2,1)}, bf16[32,32,128]{2,1,0:T(8,128)(2,1)}) custom-call(bf16[128,2,8,128]{3,2,1,0:T(8,128)(2,1)S(1)} %all_to_all.38.got, bf16[8,128,128]{2,1,0:T(8,128)(2,1)S(1)} %get-tuple-element.48.zn_in.zn, f32[8,512,128]{2,1,0:T(8,128)S(1)} %shard_map.147.slopes, f32[16,128]{1,0:T(8,128)S(1)} %get-tuple-element.49.both_gains, ...), custom_call_target="tpu_custom_call" | custom-call | flops 134217728 | bytes 2000000 | tf_op jit(solution)/shard_map/pallas_call | solution.py:268
  117.2 5.3 %all-to-all-start.4 = ((bf16[32,32,128]{2,1,0:T(8,128)(2,1)}), bf16[32,32,128]{2,1,0:T(8,128)(2,1)S(1)}, u32[]{:S(2)}, u32[]{:S(2)}) async-start(bf16[32,32,128]{2,1,0:T(8,128)(2,1)} %get-tuple-element.69), calls=%async_computation.4 | async-start | bytes 524288 | tf_op jit(solution)/shard_map/all_to_all | solution.py:302
  122.5 0.0 copy-done.2
  122.5 0.0 copy-done.3
  122.5 1.2 copy-done.1
  123.7 2.5 %shard_map.153 = f32[4,8,32,128]{3,2,1,0:T(8,128)} custom-call(bf16[8,512,128]{2,1,0:T(8,128)(2,1)S(1)} %copy-done.1, bf16[4,8,32,128]{3,2,1,0:T(8,128)(2,1)S(1)} %bitcast.21, f32[16,128]{1,0:T(8,128)S(1)} %get-tuple-element.49.both_gains, bf16[512,128]{1,0:T(8,128)(2,1)S(1)} %get-tuple-element.50.w_t, f32[8,128,128]{2,1,0:T(8,128)S(1)} %copy-done.2), custom_call_target="tpu_custom_call" | custom-call | flops 134217728 | bytes 2000000 | tf_op jit(solution)/shard_map/pallas_call | solution.py:268
  126.2 5.2 %all-to-all-done.4.parts = bf16[32,32,128]{2,1,0:T(8,128)(2,1)S(1)} async-done(((bf16[32,32,128]{2,1,0:T(8,128)(2,1)}), bf16[32,32,128]{2,1,0:T(8,128)(2,1)S(1)}, u32[]{:S(2)}, u32[]{:S(2)}) %all-to-all-start.4) | async-done | bytes 262176 | tf_op jit(solution)/shard_map/all_to_all | solution.py:302
  131.5 9.5 %all_to_all.39.parts = bf16[8,32,128]{2,1,0:T(8,128)(2,1)S(1)} all-to-all(bf16[8,32,128]{2,1,0:T(8,128)(2,1)S(1)} %shard_map.154), channel_id=1, replica_groups={{0,32,4,36,8,40,12,44},{1,33,5,37,9,41,13,45},{2,34,6,38,10,42,14,46},{..., dimensions={0} | all-to-all | bytes 131072 | tf_op jit(solution)/shard_map/all_to_all | solution.py:302
  141.0 14.0 %all_to_all.40.got = bf16[32,32,128]{2,1,0:T(8,128)(2,1)S(1)} all-to-all(bf16[32,32,128]{2,1,0:T(8,128)(2,1)S(1)} %shard_map.155), channel_id=1, replica_groups={{0,1,2,3,16,17,18,19,64,65,66,67,80,81,82,83,128,129,130,131,144,145,14..., dimensions={0} | all-to-all | bytes 524288 | tf_op jit(solution)/shard_map/all_to_all | solution.py:302
  155.1 0.8 shard_map.156
  (5 shorter events, 0.1 us)
Async XLA Ops:
  0.6 41.1 %copy-start.5 = (bf16[128,128]{1,0:T(8,128)(2,1)S(1)}, bf16[128,128]{1,0:T(8,128)(2,1)}, u32[]{:S(2)}) copy-start(bf16[128,128]{1,0:T(8,128)(2,1)} %w_out.3) | copy-start | bytes 98308
  0.6 41.1 %copy-start.4 = (bf16[128,128]{1,0:T(8,128)(2,1)S(1)}, bf16[128,128]{1,0:T(8,128)(2,1)}, u32[]{:S(2)}) copy-start(bf16[128,128]{1,0:T(8,128)(2,1)} %w_gate.3) | copy-start | bytes 98308
  0.7 41.0 %copy-start = (bf16[32,32,128]{2,1,0:T(8,128)(2,1)S(1)}, bf16[32,32,128]{2,1,0:T(8,128)(2,1)}, u32[]{:S(2)}) copy-start(bf16[32,32,128]{2,1,0:T(8,128)(2,1)} %param.10) | copy-start | bytes 786436
  38.6 4.6 %collective-permute-start = (f32[8,32,512]{2,1,0:T(8,128)S(1)}, f32[8,32,512]{2,1,0:T(8,128)S(1)}, u32[]{:S(2)}, u32[]{:S(2)}) collective-permute-start(f32[8,32,512]{2,1,0:T(8,128)S(1)} %get-tuple-element.47), channel_id=1, source_target_pairs={{0,16},{16,0},{32,48},{48,32},{64,80},{80,64},{96,112},{112,96},{1... | collective-permute-start | bytes 1572872 | tf_op jit(solution)/shard_map/ppermute | solution.py:306
  82.8 6.0 %collective-permute-start.1 = (bf16[128,8,128]{2,1,0:T(8,128)(2,1)S(1)}, bf16[128,8,128]{2,1,0:T(8,128)(2,1)S(1)}, u32[]{:S(2)}, u32[]{:S(2)}) collective-permute-start(bf16[128,8,128]{2,1,0:T(8,128)(2,1)S(1)} %all_to_all.37), channel_id=1, source_target_pairs={{0,16},{16,0},{32,48},{48,32},{64,80},{80,64},{96,112},{112,96},{1... | collective-permute-start | bytes 786440 | tf_op jit(solution)/shard_map/ppermute | solution.py:306
  115.3 7.2 %copy-start.2 = (f32[8,128,128]{2,1,0:T(8,128)S(1)}, f32[8,128,128]{2,1,0:T(8,128)}, u32[]{:S(2)}) copy-start(f32[8,128,128]{2,1,0:T(8,128)} %get-tuple-element.71.dzn_in) | copy-start | bytes 1572868
  115.3 7.2 %copy-start.3 = (bf16[32,32,128]{2,1,0:T(8,128)(2,1)S(1)}, bf16[32,32,128]{2,1,0:T(8,128)(2,1)}, u32[]{:S(2)}) copy-start(bf16[32,32,128]{2,1,0:T(8,128)(2,1)} %param.9) | copy-start | bytes 786436
  117.2 14.3 %all-to-all-start.4 = ((bf16[32,32,128]{2,1,0:T(8,128)(2,1)}), bf16[32,32,128]{2,1,0:T(8,128)(2,1)S(1)}, u32[]{:S(2)}, u32[]{:S(2)}) async-start(bf16[32,32,128]{2,1,0:T(8,128)(2,1)} %get-tuple-element.69), calls=%async_computation.4 | async-start | bytes 524288 | tf_op jit(solution)/shard_map/all_to_all | solution.py:302
  122.5 1.2 copy-start.1

commit v5 on v4

--- a/solution.py
+++ b/solution.py
@@ -167,7 +167,7 @@
     dx_out[...] = dx_all[...].astype(BF16)
 
 
-def output_grads_kernel(xn_in, cot, zn, w_gate, w_out, both_gains, update, dzn, grads, gains):
+def output_grads_kernel(xn_in, cot, zn, w_gate, w_out, both_gains, grads, gains):
     out_sum = jnp.zeros((128, 128), F32)
     gate_sum = jnp.zeros((128, 128), F32)
     for t in range(8):
@@ -176,11 +176,9 @@
         gate = jax.nn.sigmoid(dot(zn[t], w_gate[...], NN))
         dy = group(cot, t).astype(F32)
         dout = (dy * gate).astype(BF16)
-        update[:, t] = (gate * outp).astype(BF16).reshape(4, 32, 128)
         dgpre = (dy * outp * gate * (1.0 - gate)).astype(BF16)
         out_sum += dot(xn, dout, NN)
         gate_sum += dot(dgpre, zn[t], TN)
-        dzn[t] = dot(dgpre, w_gate[...], NT)
     grads[:128] = out_sum
     grads[128:] = gate_sum
     column = jnp.sum(out_sum * w_out[...].astype(F32), axis=1, keepdims=True) / column_of(both_gains[8:9])
@@ -228,10 +226,14 @@
     ).astype(BF16)
 
 
-def input_kernel(dproj, pair, both_gains, w_t, dzn_in, grad_pair):
-    for t in range(8):
+def input_kernel(dproj, pair, both_gains, w_t, xn_in, cot, zn, w_gate, w_out, grad_pair, update):
+    for t in range(8):
+        outp = dot(xn_in[t], w_out[...], TN)
+        gate = jax.nn.sigmoid(dot(zn[t], w_gate[...], NN))
+        update[:, t] = (gate * outp).astype(BF16).reshape(4, 32, 128)
+        dgpre = (group(cot, t).astype(F32) * outp * gate * (1.0 - gate)).astype(BF16)
         nhat, rstd = norm_rows(group(pair, t).astype(F32), 1)
-        dzn = dot(dproj[t], w_t[...], TN) + dzn_in[t]
+        dzn = dot(dproj[t], w_t[...], TN) + dot(dgpre, w_gate[...], NT)
         grad_pair[:, t] = norm_back(dzn * both_gains[0:1], nhat, rstd, 1).reshape(4, 32, 128)
 
 
@@ -348,16 +350,15 @@
     got = exchange(dx_chunks, SAME_CORE)
     got, xn = lax.optimization_barrier((got, xn))
     came = swap_cores(got)
-    update, dzn, early, early_gains = call(
+    early, early_gains = call(
         output_grads_kernel,
         [xn, cot4, zn, w_gate, w_out, gains],
-        [((4, 8, 32, 128), BF16), flat_wide, ((256, 128), F32), ((8, 128), F32)],
+        [((256, 128), F32), ((8, 128), F32)],
         [],
         134217728,
-        far_outputs=(0, 1),
-        near_outputs=(2, 3),
-    )
-    came, update, dzn, early, early_gains = lax.optimization_barrier((came, update, dzn, early, early_gains))
+        near_outputs=(0, 1),
+    )
+    came, early, early_gains = lax.optimization_barrier((came, early, early_gains))
     (d_chunks,) = call(
         back_product_kernel,
         [got.reshape(blocks), came.reshape(blocks), left, right],
@@ -375,10 +376,14 @@
         far_outputs=(0, 1),
     )
     parts = exchange(parts, PLANE)
-    (grad_pair,) = call(
-        input_kernel, [dproj, pair4, gains, w_t, dzn], [((4, 8, 32, 128), F32)], [], 134217728
-    )
-    parts, grad_pair = lax.optimization_barrier((parts, grad_pair))
+    grad_pair, update = call(
+        input_kernel,
+        [dproj, pair4, gains, w_t, xn, cot4, zn, w_gate, w_out],
+        [((4, 8, 32, 128), F32), ((4, 8, 32, 128), BF16)],
+        [],
+        134217728,
+    )
+    parts, grad_pair, update = lax.optimization_barrier((parts, grad_pair, update))
     parts = exchange(sum_parts(parts, 8), LINE)
     parts = exchange(sum_parts(parts, 32), PLANE)
     grad_w_in, grad_w_gate, grad_w_out, grad_gain, grad_out_gain = call(

time: 156 us -> 155 us (level)
  no operation moved by 1% of the time
where the time goes in v5:
time: 155 us
  blocking collectives  121 us (78%)
  Pallas kernels  14.8 us (10%)
  starting transfers between devices  11.7 us (8%)
  waiting for transfers between devices  5.23 us (3%)
    all_to_all x6, blocking collectives, exchange(): lax.all_to_all(chunks, AXES, 0, 0, tiled=True, axis_index_groups=groups)  121 us
    pallas_call x13, Pallas kernels, call(): pl.pallas_call(kernel, out_shape=[pltpu.HBM(shape, dtype) if n in far_out...  14.8 us
    ppermute x2, starting transfers between devices, swap_cores(): return lax.ppermute(array, 'row', [(row, row ^ 1) for row in range(16)])  6.36 us
    all_to_all x1, starting transfers between devices, exchange(): lax.all_to_all(chunks, AXES, 0, 0, tiled=True, axis_index_groups=groups)  5.31 us
    all_to_all x1, waiting for transfers between devices, exchange(): lax.all_to_all(chunks, AXES, 0, 0, tiled=True, axis_index_groups=groups)  5.05 us
  transfers between devices with their start and end apart: 3, of which 2 were waited for; matrix products, arithmetic and copies ran while one was open for 0% of the time, Pallas kernels for 4%

profile of v5, /device:TPU:1, one launch (start us, length us, event | category | flops | bytes accessed | tf_op | source)
XLA Modules:
  0.0 155.0 jit_solution(2496541091603654175)
XLA Ops:
  0.6 0.0 copy-start.3
  0.6 0.0 copy-start.2
  0.7 0.0 copy-start
  0.7 2.6 %shard_map.144 = (bf16[128,2,8,128]{3,2,1,0:T(8,128)(2,1)S(1)}, bf16[8,128,128]{2,1,0:T(8,128)(2,1)S(1)}, f32[8,128]{1,0:T(8,128)S(1)}, bf16[512,128]{1,0:T(8,128)(2,1)S(1)}, f32[16,128]{1,0:T(8,128)S(1)}) custom-call(bf16[4,8,32,128]{3,2,1,0:T(8,128)(2,1)} %bitcast.21, f32[1,128]{1,0:T(1,128)} %bitcast.27, s32[4,128]{1,0:T(4,128)} %bitcast.26, ...), custom_call_target="tpu_custom_call" | custom-call | flops 134217728 | bytes 2000000 | tf_op jit(solution)/shard_map/pallas_call | solution.py:270
  3.3 34.4 %all_to_all.35 = bf16[128,2,8,128]{3,2,1,0:T(8,128)(2,1)S(1)} all-to-all(bf16[128,2,8,128]{3,2,1,0:T(8,128)(2,1)S(1)} %get-tuple-element.42), channel_id=1, replica_groups={{0,1,2,3,4,5,6,7,8,9,10,11,12,13,14,15,32,33,34,35,36,37,38,39,40,41,42..., dimensions={0} | all-to-all | bytes 1048576 | tf_op jit(solution)/shard_map/all_to_all | solution.py:304
  37.7 1.0 shard_map.145
  38.6 3.1 %collective-permute-start = (f32[8,32,512]{2,1,0:T(8,128)S(1)}, f32[8,32,512]{2,1,0:T(8,128)S(1)}, u32[]{:S(2)}, u32[]{:S(2)}) collective-permute-start(f32[8,32,512]{2,1,0:T(8,128)S(1)} %get-tuple-element.46), channel_id=1, source_target_pairs={{0,16},{16,0},{32,48},{48,32},{64,80},{80,64},{96,112},{112,96},{1... | collective-permute-start | bytes 1572872 | tf_op jit(solution)/shard_map/ppermute | solution.py:308
  41.7 0.0 copy-done.3
  41.7 0.0 copy-done.2
  41.7 0.0 copy-done
  41.7 0.9 shard_map.146.e_in
  42.6 0.5 shard_map.147.slopes
  43.1 0.2 collective-permute-done.came
  43.2 0.4 shard_map.148
  43.6 18.9 %all_to_all.36.got = bf16[128,8,128]{2,1,0:T(8,128)(2,1)S(1)} all-to-all(bf16[128,8,128]{2,1,0:T(8,128)(2,1)S(1)} %bitcast.19), channel_id=1, replica_groups={{0,1,2,3,4,5,6,7,8,9,10,11,12,13,14,15,32,33,34,35,36,37,38,39,40,41,42..., dimensions={0} | all-to-all | bytes 524288 | tf_op jit(solution)/shard_map/all_to_all | solution.py:304
  62.5 0.9 shard_map.149
  63.5 19.3 %all_to_all.37 = bf16[128,8,128]{2,1,0:T(8,128)(2,1)S(1)} all-to-all(bf16[128,8,128]{2,1,0:T(8,128)(2,1)S(1)} %get-tuple-element.53), channel_id=1, replica_groups={{0,1,2,3,4,5,6,7,8,9,10,11,12,13,14,15,32,33,34,35,36,37,38,39,40,41,42..., dimensions={0} | all-to-all | bytes 524288 | tf_op jit(solution)/shard_map/all_to_all | solution.py:304
  82.8 3.3 %collective-permute-start.1 = (bf16[128,8,128]{2,1,0:T(8,128)(2,1)S(1)}, bf16[128,8,128]{2,1,0:T(8,128)(2,1)S(1)}, u32[]{:S(2)}, u32[]{:S(2)}) collective-permute-start(bf16[128,8,128]{2,1,0:T(8,128)(2,1)S(1)} %all_to_all.37), channel_id=1, source_target_pairs={{0,16},{16,0},{32,48},{48,32},{64,80},{80,64},{96,112},{112,96},{1... | collective-permute-start | bytes 786440 | tf_op jit(solution)/shard_map/ppermute | solution.py:308
  86.1 1.7 %shard_map.150 = (f32[256,128]{1,0:T(8,128)S(1)}, f32[8,128]{1,0:T(8,128)S(1)}) custom-call(bf16[8,128,128]{2,1,0:T(8,128)(2,1)S(1)} %get-tuple-element.56.xn_in, bf16[4,8,32,128]{3,2,1,0:T(8,128)(2,1)S(1)} %bitcast.15, bf16[8,128,128]{2,1,0:T(8,128)(2,1)S(1)} %get-tuple-element.47.zn_in.zn, bf16[128,128]{1,0:T(8,128)(2,1)S(1)} %copy-done.2, ...), custom_call_target="tpu_custom_call" | custom-call | flops 134217728 | bytes 2000000 | tf_op jit(solution)/shard_map/pallas_call | solution.py:270
  87.8 0.0 collective-permute-done.1
  87.8 1.4 shard_map.151
  89.2 25.1 %all_to_all.38.got = bf16[128,2,8,128]{3,2,1,0:T(8,128)(2,1)S(1)} all-to-all(bf16[128,2,8,128]{3,2,1,0:T(8,128)(2,1)S(1)} %bitcast.17), channel_id=1, replica_groups={{0,1,2,3,4,5,6,7,8,9,10,11,12,13,14,15,32,33,34,35,36,37,38,39,40,41,42..., dimensions={0} | all-to-all | bytes 1048576 | tf_op jit(solution)/shard_map/all_to_all | solution.py:304
  114.3 1.9 %shard_map.152 = (bf16[8,512,128]{2,1,0:T(8,128)(2,1)}, bf16[32,32,128]{2,1,0:T(8,128)(2,1)}) custom-call(bf16[128,2,8,128]{3,2,1,0:T(8,128)(2,1)S(1)} %all_to_all.38.got, bf16[8,128,128]{2,1,0:T(8,128)(2,1)S(1)} %get-tuple-element.47.zn_in.zn, f32[8,512,128]{2,1,0:T(8,128)S(1)} %shard_map.147.slopes, f32[16,128]{1,0:T(8,128)S(1)} %get-tuple-element.48.both_gains, ...), custom_call_target="tpu_custom_call" | custom-call | flops 134217728 | bytes 2000000 | tf_op jit(solution)/shard_map/pallas_call | solution.py:270
  116.2 5.3 %all-to-all-start.4 = ((bf16[32,32,128]{2,1,0:T(8,128)(2,1)}), bf16[32,32,128]{2,1,0:T(8,128)(2,1)S(1)}, u32[]{:S(2)}, u32[]{:S(2)}) async-start(bf16[32,32,128]{2,1,0:T(8,128)(2,1)} %get-tuple-element.65), calls=%async_computation.4 | async-start | bytes 524288 | tf_op jit(solution)/shard_map/all_to_all | solution.py:304
  121.5 0.0 copy-done.4
  121.5 0.0 copy-start.1
  121.5 1.2 copy-done.1
  122.7 2.7 %shard_map.153 = (f32[4,8,32,128]{3,2,1,0:T(8,128)}, bf16[4,8,32,128]{3,2,1,0:T(8,128)(2,1)}) custom-call(bf16[8,512,128]{2,1,0:T(8,128)(2,1)S(1)} %copy-done.1, bf16[4,8,32,128]{3,2,1,0:T(8,128)(2,1)S(1)} %bitcast.22, f32[16,128]{1,0:T(8,128)S(1)} %get-tuple-element.48.both_gains, bf16[512,128]{1,0:T(8,128)(2,1)S(1)} %get-tuple-element.49.w_t, ...), custom_call_target="tpu_custom_call" | custom-call | flops 134217728 | bytes 2000000 | tf_op jit(solution)/shard_map/pallas_call | solution.py:270
  125.4 5.0 %all-to-all-done.4.parts = bf16[32,32,128]{2,1,0:T(8,128)(2,1)S(1)} async-done(((bf16[32,32,128]{2,1,0:T(8,128)(2,1)}), bf16[32,32,128]{2,1,0:T(8,128)(2,1)S(1)}, u32[]{:S(2)}, u32[]{:S(2)}) %all-to-all-start.4) | async-done | bytes 262176 | tf_op jit(solution)/shard_map/all_to_all | solution.py:304
  130.5 9.5 %all_to_all.39.parts = bf16[8,32,128]{2,1,0:T(8,128)(2,1)S(1)} all-to-all(bf16[8,32,128]{2,1,0:T(8,128)(2,1)S(1)} %shard_map.154), channel_id=1, replica_groups={{0,32,4,36,8,40,12,44},{1,33,5,37,9,41,13,45},{2,34,6,38,10,42,14,46},{..., dimensions={0} | all-to-all | bytes 131072 | tf_op jit(solution)/shard_map/all_to_all | solution.py:304
  140.1 14.0 %all_to_all.40.got = bf16[32,32,128]{2,1,0:T(8,128)(2,1)S(1)} all-to-all(bf16[32,32,128]{2,1,0:T(8,128)(2,1)S(1)} %shard_map.155), channel_id=1, replica_groups={{0,1,2,3,16,17,18,19,64,65,66,67,80,81,82,83,128,129,130,131,144,145,14..., dimensions={0} | all-to-all | bytes 524288 | tf_op jit(solution)/shard_map/all_to_all | solution.py:304
  154.1 0.8 shard_map.156
  (3 shorter events, 0.1 us)
Async XLA Ops:
  0.6 41.1 %copy-start.3 = (bf16[128,128]{1,0:T(8,128)(2,1)S(1)}, bf16[128,128]{1,0:T(8,128)(2,1)}, u32[]{:S(2)}) copy-start(bf16[128,128]{1,0:T(8,128)(2,1)} %w_out.5) | copy-start | bytes 98308
  0.6 41.1 %copy-start.2 = (bf16[128,128]{1,0:T(8,128)(2,1)S(1)}, bf16[128,128]{1,0:T(8,128)(2,1)}, u32[]{:S(2)}) copy-start(bf16[128,128]{1,0:T(8,128)(2,1)} %w_gate.5) | copy-start | bytes 98308
  0.7 41.0 %copy-start = (bf16[32,32,128]{2,1,0:T(8,128)(2,1)S(1)}, bf16[32,32,128]{2,1,0:T(8,128)(2,1)}, u32[]{:S(2)}) copy-start(bf16[32,32,128]{2,1,0:T(8,128)(2,1)} %param.10) | copy-start | bytes 786436
  38.6 4.6 %collective-permute-start = (f32[8,32,512]{2,1,0:T(8,128)S(1)}, f32[8,32,512]{2,1,0:T(8,128)S(1)}, u32[]{:S(2)}, u32[]{:S(2)}) collective-permute-start(f32[8,32,512]{2,1,0:T(8,128)S(1)} %get-tuple-element.46), channel_id=1, source_target_pairs={{0,16},{16,0},{32,48},{48,32},{64,80},{80,64},{96,112},{112,96},{1... | collective-permute-start | bytes 1572872 | tf_op jit(solution)/shard_map/ppermute | solution.py:308
  82.8 5.0 %collective-permute-start.1 = (bf16[128,8,128]{2,1,0:T(8,128)(2,1)S(1)}, bf16[128,8,128]{2,1,0:T(8,128)(2,1)S(1)}, u32[]{:S(2)}, u32[]{:S(2)}) collective-permute-start(bf16[128,8,128]{2,1,0:T(8,128)(2,1)S(1)} %all_to_all.37), channel_id=1, source_target_pairs={{0,16},{16,0},{32,48},{48,32},{64,80},{80,64},{96,112},{112,96},{1... | collective-permute-start | bytes 786440 | tf_op jit(solution)/shard_map/ppermute | solution.py:308
  114.3 7.2 %copy-start.4 = (bf16[32,32,128]{2,1,0:T(8,128)(2,1)S(1)}, bf16[32,32,128]{2,1,0:T(8,128)(2,1)}, u32[]{:S(2)}) copy-start(bf16[32,32,128]{2,1,0:T(8,128)(2,1)} %param.9) | copy-start | bytes 786436
  116.2 14.3 %all-to-all-start.4 = ((bf16[32,32,128]{2,1,0:T(8,128)(2,1)}), bf16[32,32,128]{2,1,0:T(8,128)(2,1)S(1)}, u32[]{:S(2)}, u32[]{:S(2)}) async-start(bf16[32,32,128]{2,1,0:T(8,128)(2,1)} %get-tuple-element.65), calls=%async_computation.4 | async-start | bytes 524288 | tf_op jit(solution)/shard_map/all_to_all | solution.py:304
  121.5 1.2 copy-start.1

commit v6 on v5

--- a/solution.py
+++ b/solution.py
@@ -144,15 +144,13 @@
     x_all[...] = dot(left[...], right[...], TN).reshape(8, 2, 32, 512)
     core = lax.axis_index("row") % 2
     keep[...] = x_all[:, core]
-    send[...] = x_all[:, 1 - core]
+    send[...] = x_all[:, 1 - core].astype(BF16)
 
 
 def product_sum_kernel(keep, came, x_out):
+    both = keep[...] + came[...].astype(F32)
     for hi in range(4):
-        lanes = pl.ds(128 * hi, 128)
-        u = swap_segments(
-            [(keep[:, 8 * m : 8 * m + 8, lanes] + came[:, 8 * m : 8 * m + 8, lanes]).reshape(64, 128) for m in range(4)]
-        )
+        u = swap_segments([both[:, 8 * m : 8 * m + 8, 128 * hi : 128 * hi + 128].reshape(64, 128) for m in range(4)])
         for lo in range(4):
             x_out[:, hi, lo] = u[lo].reshape(8, 8, 128).astype(BF16)
 
@@ -334,7 +332,7 @@
     keep, send, left, right = call(
         product_kernel,
         [got],
-        [((8, 32, 512), F32), ((8, 32, 512), F32), rows, rows],
+        [((8, 32, 512), F32), ((8, 32, 512), BF16), rows, rows],
         [(8, 2, 32, 512)],
         134217728,
     )

time: 155 us -> 155 us (level)
  transfers between devices with their start and end apart: 3 -> 3, of which waited for: 2 -> 1; matrix products, arithmetic and copies ran while one was open for 0% -> 0% of each run, Pallas kernels for 4% -> 4%
where the time goes in v6:
time: 155 us
  blocking collectives  121 us (78%)
  Pallas kernels  14.8 us (10%)
  starting transfers between devices  11.7 us (8%)
  waiting for transfers between devices  5.06 us (3%)
    all_to_all x6, blocking collectives, exchange(): lax.all_to_all(chunks, AXES, 0, 0, tiled=True, axis_index_groups=groups)  121 us
    pallas_call x13, Pallas kernels, call(): pl.pallas_call(kernel, out_shape=[pltpu.HBM(shape, dtype) if n in far_out...  14.8 us
    ppermute x2, starting transfers between devices, swap_cores(): return lax.ppermute(array, 'row', [(row, row ^ 1) for row in range(16)])  6.35 us
    all_to_all x1, starting transfers between devices, exchange(): lax.all_to_all(chunks, AXES, 0, 0, tiled=True, axis_index_groups=groups)  5.32 us
    all_to_all x1, waiting for transfers between devices, exchange(): lax.all_to_all(chunks, AXES, 0, 0, tiled=True, axis_index_groups=groups)  5.05 us
  transfers between devices with their start and end apart: 3, of which 1 were waited for; matrix products, arithmetic and copies ran while one was open for 0% of the time, Pallas kernels for 4%

profile of v6, /device:TPU:1, one launch (start us, length us, event | category | flops | bytes accessed | tf_op | source)
XLA Modules:
  0.0 154.8 jit_solution(12131091109932139309)
XLA Ops:
  0.6 0.0 copy-start.3
  0.6 0.0 copy-start.2
  0.7 0.0 copy-start
  0.7 2.6 %shard_map.144 = (bf16[128,2,8,128]{3,2,1,0:T(8,128)(2,1)S(1)}, bf16[8,128,128]{2,1,0:T(8,128)(2,1)S(1)}, f32[8,128]{1,0:T(8,128)S(1)}, bf16[512,128]{1,0:T(8,128)(2,1)S(1)}, f32[16,128]{1,0:T(8,128)S(1)}) custom-call(bf16[4,8,32,128]{3,2,1,0:T(8,128)(2,1)} %bitcast.21, f32[1,128]{1,0:T(1,128)} %bitcast.27, s32[4,128]{1,0:T(4,128)} %bitcast.26, ...), custom_call_target="tpu_custom_call" | custom-call | flops 134217728 | bytes 2000000 | tf_op jit(solution)/shard_map/pallas_call | solution.py:268
  3.3 34.4 %all_to_all.35 = bf16[128,2,8,128]{3,2,1,0:T(8,128)(2,1)S(1)} all-to-all(bf16[128,2,8,128]{3,2,1,0:T(8,128)(2,1)S(1)} %get-tuple-element.42), channel_id=1, replica_groups={{0,1,2,3,4,5,6,7,8,9,10,11,12,13,14,15,32,33,34,35,36,37,38,39,40,41,42..., dimensions={0} | all-to-all | bytes 1048576 | tf_op jit(solution)/shard_map/all_to_all | solution.py:302
  37.7 1.0 shard_map.145
  38.6 3.1 %collective-permute-start = (bf16[8,32,512]{2,1,0:T(8,128)(2,1)S(1)}, bf16[8,32,512]{2,1,0:T(8,128)(2,1)S(1)}, u32[]{:S(2)}, u32[]{:S(2)}) collective-permute-start(bf16[8,32,512]{2,1,0:T(8,128)(2,1)S(1)} %get-tuple-element.46), channel_id=1, source_target_pairs={{0,16},{16,0},{32,48},{48,32},{64,80},{80,64},{96,112},{112,96},{1... | collective-permute-start | bytes 786440 | tf_op jit(solution)/shard_map/ppermute | solution.py:306
  41.7 0.0 copy-done.3
  41.7 0.0 copy-done.2
  41.7 0.0 copy-done
  41.7 0.9 shard_map.146.e_in
  42.6 0.5 shard_map.147.slopes
  43.1 0.0 collective-permute-done.came
  43.1 0.4 shard_map.148
  43.5 19.4 %all_to_all.36.got = bf16[128,8,128]{2,1,0:T(8,128)(2,1)S(1)} all-to-all(bf16[128,8,128]{2,1,0:T(8,128)(2,1)S(1)} %bitcast.20), channel_id=1, replica_groups={{0,1,2,3,4,5,6,7,8,9,10,11,12,13,14,15,32,33,34,35,36,37,38,39,40,41,42..., dimensions={0} | all-to-all | bytes 524288 | tf_op jit(solution)/shard_map/all_to_all | solution.py:302
  62.9 0.9 shard_map.149
  63.8 18.8 %all_to_all.37 = bf16[128,8,128]{2,1,0:T(8,128)(2,1)S(1)} all-to-all(bf16[128,8,128]{2,1,0:T(8,128)(2,1)S(1)} %get-tuple-element.53), channel_id=1, replica_groups={{0,1,2,3,4,5,6,7,8,9,10,11,12,13,14,15,32,33,34,35,36,37,38,39,40,41,42..., dimensions={0} | all-to-all | bytes 524288 | tf_op jit(solution)/shard_map/all_to_all | solution.py:302
  82.6 3.3 %collective-permute-start.1 = (bf16[128,8,128]{2,1,0:T(8,128)(2,1)S(1)}, bf16[128,8,128]{2,1,0:T(8,128)(2,1)S(1)}, u32[]{:S(2)}, u32[]{:S(2)}) collective-permute-start(bf16[128,8,128]{2,1,0:T(8,128)(2,1)S(1)} %all_to_all.37), channel_id=1, source_target_pairs={{0,16},{16,0},{32,48},{48,32},{64,80},{80,64},{96,112},{112,96},{1... | collective-permute-start | bytes 786440 | tf_op jit(solution)/shard_map/ppermute | solution.py:306
  85.9 1.7 %shard_map.150 = (f32[256,128]{1,0:T(8,128)S(1)}, f32[8,128]{1,0:T(8,128)S(1)}) custom-call(bf16[8,128,128]{2,1,0:T(8,128)(2,1)S(1)} %get-tuple-element.56.xn_in, bf16[4,8,32,128]{3,2,1,0:T(8,128)(2,1)S(1)} %bitcast.15, bf16[8,128,128]{2,1,0:T(8,128)(2,1)S(1)} %get-tuple-element.47.zn_in.zn, bf16[128,128]{1,0:T(8,128)(2,1)S(1)} %copy-done.2, ...), custom_call_target="tpu_custom_call" | custom-call | flops 134217728 | bytes 2000000 | tf_op jit(solution)/shard_map/pallas_call | solution.py:268
  87.6 0.0 collective-permute-done.1
  87.6 1.4 shard_map.151
  89.0 25.1 %all_to_all.38.got = bf16[128,2,8,128]{3,2,1,0:T(8,128)(2,1)S(1)} all-to-all(bf16[128,2,8,128]{3,2,1,0:T(8,128)(2,1)S(1)} %bitcast.17), channel_id=1, replica_groups={{0,1,2,3,4,5,6,7,8,9,10,11,12,13,14,15,32,33,34,35,36,37,38,39,40,41,42..., dimensions={0} | all-to-all | bytes 1048576 | tf_op jit(solution)/shard_map/all_to_all | solution.py:302
  114.1 1.9 %shard_map.152 = (bf16[8,512,128]{2,1,0:T(8,128)(2,1)}, bf16[32,32,128]{2,1,0:T(8,128)(2,1)}) custom-call(bf16[128,2,8,128]{3,2,1,0:T(8,128)(2,1)S(1)} %all_to_all.38.got, bf16[8,128,128]{2,1,0:T(8,128)(2,1)S(1)} %get-tuple-element.47.zn_in.zn, f32[8,512,128]{2,1,0:T(8,128)S(1)} %shard_map.147.slopes, f32[16,128]{1,0:T(8,128)S(1)} %get-tuple-element.48.both_gains, ...), custom_call_target="tpu_custom_call" | custom-call | flops 134217728 | bytes 2000000 | tf_op jit(solution)/shard_map/pallas_call | solution.py:268
  116.0 5.3 %all-to-all-start.4 = ((bf16[32,32,128]{2,1,0:T(8,128)(2,1)}), bf16[32,32,128]{2,1,0:T(8,128)(2,1)S(1)}, u32[]{:S(2)}, u32[]{:S(2)}) async-start(bf16[32,32,128]{2,1,0:T(8,128)(2,1)} %get-tuple-element.65), calls=%async_computation.4 | async-start | bytes 524288 | tf_op jit(solution)/shard_map/all_to_all | solution.py:302
  121.3 0.0 copy-done.4
  121.3 0.0 copy-start.1
  121.4 1.2 copy-done.1
  122.6 2.7 %shard_map.153 = (f32[4,8,32,128]{3,2,1,0:T(8,128)}, bf16[4,8,32,128]{3,2,1,0:T(8,128)(2,1)}) custom-call(bf16[8,512,128]{2,1,0:T(8,128)(2,1)S(1)} %copy-done.1, bf16[4,8,32,128]{3,2,1,0:T(8,128)(2,1)S(1)} %bitcast.22, f32[16,128]{1,0:T(8,128)S(1)} %get-tuple-element.48.both_gains, bf16[512,128]{1,0:T(8,128)(2,1)S(1)} %get-tuple-element.49.w_t, ...), custom_call_target="tpu_custom_call" | custom-call | flops 134217728 | bytes 2000000 | tf_op jit(solution)/shard_map/pallas_call | solution.py:268
  125.3 5.0 %all-to-all-done.4.parts = bf16[32,32,128]{2,1,0:T(8,128)(2,1)S(1)} async-done(((bf16[32,32,128]{2,1,0:T(8,128)(2,1)}), bf16[32,32,128]{2,1,0:T(8,128)(2,1)S(1)}, u32[]{:S(2)}, u32[]{:S(2)}) %all-to-all-start.4) | async-done | bytes 262176 | tf_op jit(solution)/shard_map/all_to_all | solution.py:302
  130.4 9.5 %all_to_all.39.parts = bf16[8,32,128]{2,1,0:T(8,128)(2,1)S(1)} all-to-all(bf16[8,32,128]{2,1,0:T(8,128)(2,1)S(1)} %shard_map.154), channel_id=1, replica_groups={{0,32,4,36,8,40,12,44},{1,33,5,37,9,41,13,45},{2,34,6,38,10,42,14,46},{..., dimensions={0} | all-to-all | bytes 131072 | tf_op jit(solution)/shard_map/all_to_all | solution.py:302
  139.9 14.0 %all_to_all.40.got = bf16[32,32,128]{2,1,0:T(8,128)(2,1)S(1)} all-to-all(bf16[32,32,128]{2,1,0:T(8,128)(2,1)S(1)} %shard_map.155), channel_id=1, replica_groups={{0,1,2,3,16,17,18,19,64,65,66,67,80,81,82,83,128,129,130,131,144,145,14..., dimensions={0} | all-to-all | bytes 524288 | tf_op jit(solution)/shard_map/all_to_all | solution.py:302
  154.0 0.8 shard_map.156
  (3 shorter events, 0.1 us)
Async XLA Ops:
  0.6 41.1 %copy-start.3 = (bf16[128,128]{1,0:T(8,128)(2,1)S(1)}, bf16[128,128]{1,0:T(8,128)(2,1)}, u32[]{:S(2)}) copy-start(bf16[128,128]{1,0:T(8,128)(2,1)} %w_out.5) | copy-start | bytes 98308
  0.6 41.1 %copy-start.2 = (bf16[128,128]{1,0:T(8,128)(2,1)S(1)}, bf16[128,128]{1,0:T(8,128)(2,1)}, u32[]{:S(2)}) copy-start(bf16[128,128]{1,0:T(8,128)(2,1)} %w_gate.5) | copy-start | bytes 98308
  0.7 41.1 %copy-start = (bf16[32,32,128]{2,1,0:T(8,128)(2,1)S(1)}, bf16[32,32,128]{2,1,0:T(8,128)(2,1)}, u32[]{:S(2)}) copy-start(bf16[32,32,128]{2,1,0:T(8,128)(2,1)} %param.10) | copy-start | bytes 786436
  38.6 4.4 %collective-permute-start = (bf16[8,32,512]{2,1,0:T(8,128)(2,1)S(1)}, bf16[8,32,512]{2,1,0:T(8,128)(2,1)S(1)}, u32[]{:S(2)}, u32[]{:S(2)}) collective-permute-start(bf16[8,32,512]{2,1,0:T(8,128)(2,1)S(1)} %get-tuple-element.46), channel_id=1, source_target_pairs={{0,16},{16,0},{32,48},{48,32},{64,80},{80,64},{96,112},{112,96},{1... | collective-permute-start | bytes 786440 | tf_op jit(solution)/shard_map/ppermute | solution.py:306
  82.6 5.0 %collective-permute-start.1 = (bf16[128,8,128]{2,1,0:T(8,128)(2,1)S(1)}, bf16[128,8,128]{2,1,0:T(8,128)(2,1)S(1)}, u32[]{:S(2)}, u32[]{:S(2)}) collective-permute-start(bf16[128,8,128]{2,1,0:T(8,128)(2,1)S(1)} %all_to_all.37), channel_id=1, source_target_pairs={{0,16},{16,0},{32,48},{48,32},{64,80},{80,64},{96,112},{112,96},{1... | collective-permute-start | bytes 786440 | tf_op jit(solution)/shard_map/ppermute | solution.py:306
  114.1 7.2 %copy-start.4 = (bf16[32,32,128]{2,1,0:T(8,128)(2,1)S(1)}, bf16[32,32,128]{2,1,0:T(8,128)(2,1)}, u32[]{:S(2)}) copy-start(bf16[32,32,128]{2,1,0:T(8,128)(2,1)} %param.9) | copy-start | bytes 786436
  116.0 14.3 %all-to-all-start.4 = ((bf16[32,32,128]{2,1,0:T(8,128)(2,1)}), bf16[32,32,128]{2,1,0:T(8,128)(2,1)S(1)}, u32[]{:S(2)}, u32[]{:S(2)}) async-start(bf16[32,32,128]{2,1,0:T(8,128)(2,1)} %get-tuple-element.65), calls=%async_computation.4 | async-start | bytes 524288 | tf_op jit(solution)/shard_map/all_to_all | solution.py:302
  121.3 1.2 copy-start.1
